TPU v7x, 1024 devices: a whole 8x8x8 slice. The times are simulated.
1024 devices in a mesh: row: 32 (over z, x_lo, core), col: 32 (over y, x_hi).
Axes of the slice: x: 8 (x_hi: 4, x_lo: 2; x = x_hi * 2 + x_lo), y: 8, z: 8, core: 2. Of those that a mesh axis runs over, the one named last changes fastest.
Arguments:
- current_block: float32 [8, 262144], P(None, ('row', 'col')), may hold values from -6 to 6
- previous_block: float32 [8, 262144], P(None, ('row', 'col')), may hold values from -6 to 6
- beta_coupling: float32 [8, 8], replicated, may hold values from -3 to 3
- diagonal: float32 [262144], P(('row', 'col')), may hold values from 0.5 to 2
- blocks: bfloat16 [32, 32, 96, 128, 128], P('row', 'col'), may hold values from -0.0546875 to 0.0546875
- near_index: int32 [32, 32, 96], P('row', 'col'), may hold values from 0 to 63
- far_index: int32 [32, 32, 96], P('row', 'col'), may hold values from 0 to 63
- counts: int32 [32, 32], P('row', 'col'), may hold values from 32 to 96, as said below
Outputs:
- residual_block: float32 [8, 262144], P(None, ('row', 'col'))
- next_block: float32 [8, 262144], P(None, ('row', 'col'))
- coefficients: float32 [3, 8, 8], replicated
Inputs may be any that keep to these rules, and one draw needn't show every extreme that they name: `counts`: tiles hold different numbers of live slots; some tile in every draw has all 96 slots live.
All inputs are finite; a program needn't handle non-finite values.
Results may differ from a plain program's by a relative error of at most 0.002.
Values may be sent and summed in bfloat16 or wider, within the bound.
No kernel may reach another device: no remote copies, remote signals or barrier semaphores. Data moves between devices by JAX's collectives and lax.ppermute only.
A program may use at most 32 MiB of HBM per device.

v0:
```python
import jax
import jax.numpy as jnp
from jax import lax
from jax.sharding import PartitionSpec as P


def inner_products(left, right):
    return jnp.dot(left, right.T, precision=lax.Precision.HIGHEST)


def global_sum(values):
    return lax.psum(values, ("row", "col"))


def on_device(
    current_block, previous_block, beta_coupling, diagonal, blocks, near_index, far_index, counts
):
    tile_blocks = blocks[0, 0]
    near_list = near_index[0, 0]
    far_list = far_index[0, 0]
    live_count = counts[0, 0]
    vector_count = current_block.shape[0]
    block_width = tile_blocks.shape[-1]
    total_slots = tile_blocks.shape[0]
    rows_total = current_block.shape[1] * lax.axis_size("row") * lax.axis_size("col")
    live_mask = (jnp.arange(total_slots) < live_count).astype(jnp.float32)

    def apply_matrix(vectors):
        rounded = vectors.astype(jnp.bfloat16)
        row_segment = lax.all_gather(rounded, "col", axis=1, tiled=True).reshape(
            vector_count, -1, block_width
        )
        column_segment = lax.all_gather(rounded, "row", axis=1, tiled=True).reshape(
            vector_count, -1, block_width
        )
        near_total = row_segment.shape[1]
        far_total = column_segment.shape[1]
        from_far = jnp.take(column_segment, far_list, axis=1)
        from_near = jnp.take(row_segment, near_list, axis=1)
        to_near = jnp.einsum(
            "vkj,kij->vki", from_far, tile_blocks, preferred_element_type=jnp.float32
        )
        to_far = jnp.einsum(
            "vki,kij->vkj", from_near, tile_blocks, preferred_element_type=jnp.float32
        )
        pick_near = (near_list[:, None] == jnp.arange(near_total)[None, :]).astype(
            jnp.float32
        ) * live_mask[:, None]
        pick_far = (far_list[:, None] == jnp.arange(far_total)[None, :]).astype(
            jnp.float32
        ) * live_mask[:, None]
        near_part = jnp.einsum("vki,kn->vni", to_near, pick_near, precision=lax.Precision.HIGHEST)
        far_part = jnp.einsum("vkj,kn->vnj", to_far, pick_far, precision=lax.Precision.HIGHEST)
        from_rows = lax.psum_scatter(
            near_part.reshape(vector_count, -1), "col", scatter_dimension=1, tiled=True
        )
        from_columns = lax.psum_scatter(
            far_part.reshape(vector_count, -1), "row", scatter_dimension=1, tiled=True
        )
        return from_rows + from_columns + diagonal[None, :] * vectors

    product = apply_matrix(current_block) - jnp.dot(
        beta_coupling, previous_block, precision=lax.Precision.HIGHEST
    )
    alpha_one = global_sum(inner_products(current_block, product)) / rows_total
    adjusted = product - jnp.dot(alpha_one.T, current_block, precision=lax.Precision.HIGHEST)
    moment = global_sum(inner_products(adjusted, adjusted)) / rows_total
    factor_lower = jnp.linalg.cholesky(moment)
    next_block = lax.linalg.triangular_solve(factor_lower, adjusted, left_side=True, lower=True)
    second = apply_matrix(next_block) - jnp.dot(
        factor_lower.T, current_block, precision=lax.Precision.HIGHEST
    )
    alpha_two = global_sum(inner_products(next_block, second)) / rows_total
    residual_block = second - jnp.dot(alpha_two.T, next_block, precision=lax.Precision.HIGHEST)
    return (residual_block, next_block, jnp.stack([alpha_one, factor_lower, alpha_two]))


def solution(mesh):
    return jax.shard_map(
        on_device,
        mesh=mesh,
        in_specs=(
            P(None, ("row", "col")),
            P(None, ("row", "col")),
            P(),
            P(("row", "col")),
            P("row", "col", None, None, None),
            P("row", "col", None),
            P("row", "col", None),
            P("row", "col"),
        ),
        out_specs=(P(None, ("row", "col")), P(None, ("row", "col")), P()),
        check_vma=False,
    )
```

profile of v0, /device:TPU:1, one launch (start us, length us, event | category | flops | bytes accessed | tf_op | source)
XLA Modules:
  0.0 1144.1 jit_solution(12608798857799134374)
XLA Ops:
  7.2 0.8 compare_select_fusion
  8.0 0.8 compare_and_fusion
  9.5 48.5 %all_gather.12 = bf16[8,8192]{1,0:T(8,128)(2,1)S(1)} all-gather(bf16[8,256]{1,0:T(8,128)(2,1)S(1)} %convert_element_type.18), channel_id=1, replica_groups=mesh['row'=32,'col'=32] {'row'}, dimensions={1}, use_global_device_ids=true | all-gather | bytes 135168 | tf_op jit(solution)/shard_map/all_gather | solution.py:33
  59.4 1.7 fusion.6
  61.6 0.8 copy.50
  62.6 68.5 %all_gather.13 = bf16[8,8192]{1,0:T(8,128)(2,1)S(1)} all-gather(bf16[8,256]{1,0:T(8,128)(2,1)S(1)} %convert_element_type.18), channel_id=1, replica_groups=mesh['row'=32,'col'=32] {'col'}, dimensions={1}, use_global_device_ids=true | all-gather | bytes 135168 | tf_op jit(solution)/shard_map/all_gather | solution.py:30
  131.8 1.0 fusion.4
  133.2 0.9 copy.49
  134.1 147.8 %reduce-scatter.5.cloned.1.call-done = f32[8,256]{1,0:T(8,128)} async-done(((f32[8,8192]{1,0:T(8,128)}), f32[8,256]{1,0:T(8,128)}) %reduce-scatter.5.cloned.1.call-update) | async-done | bytes 8208 | tf_op jit(solution)/shard_map/reduce_scatter | solution.py:54
  281.9 125.6 %reduce-scatter.7.cloned.1.call-done = f32[8,256]{1,0:T(8,128)} async-done(((f32[8,8192]{1,0:T(8,128)}), f32[8,256]{1,0:T(8,128)}) %reduce-scatter.7.cloned.1.call-update) | async-done | bytes 8208 | tf_op jit(solution)/shard_map/reduce_scatter | solution.py:57
  407.6 0.8 convolution_subtract_fusion.3
  408.5 115.0 %psum.21 = f32[8,8]{0,1:T(8,128)S(1)} all-reduce(f32[8,8]{0,1:T(8,128)S(1)} %convolution_bitcast_fusion.4), channel_id=1, replica_groups=mesh['row'=32,'col'=32] {'row','col'}, use_global_device_ids=true, to_apply=%region_2.4 | all-reduce | flops 64 | bytes 512 | tf_op jit(solution)/shard_map/psum | solution.py:12
  523.8 110.6 %psum.22 = f32[8,8]{0,1:T(8,128)S(1)} all-reduce(f32[8,8]{0,1:T(8,128)S(1)} %fusion.70), channel_id=1, replica_groups=mesh['row'=32,'col'=32] {'row','col'}, use_global_device_ids=true, to_apply=%region_3.5 | all-reduce | flops 64 | bytes 512 | tf_op jit(solution)/shard_map/psum | solution.py:12
  637.3 33.1 %all_gather.14 = bf16[8,8192]{1,0:T(8,128)(2,1)S(1)} all-gather(bf16[8,256]{1,0:T(8,128)(2,1)S(1)} %get-tuple-element.6), channel_id=1, replica_groups=mesh['row'=32,'col'=32] {'row'}, dimensions={1}, use_global_device_ids=true | all-gather | bytes 135168 | tf_op jit(solution)/shard_map/all_gather | solution.py:33
  671.0 1.7 fusion.2
  673.3 0.8 copy.48
  674.2 65.0 %all_gather.15 = bf16[8,8192]{1,0:T(8,128)(2,1)S(1)} all-gather(bf16[8,256]{1,0:T(8,128)(2,1)S(1)} %get-tuple-element.6), channel_id=1, replica_groups=mesh['row'=32,'col'=32] {'col'}, dimensions={1}, use_global_device_ids=true | all-gather | bytes 135168 | tf_op jit(solution)/shard_map/all_gather | solution.py:30
  739.8 1.0 fusion
  741.2 0.9 copy.47
  742.2 151.9 %reduce-scatter.9.cloned.1.call-done = f32[8,256]{1,0:T(8,128)} async-done(((f32[8,8192]{1,0:T(8,128)}), f32[8,256]{1,0:T(8,128)}) %reduce-scatter.9.cloned.1.call-update) | async-done | bytes 8208 | tf_op jit(solution)/shard_map/reduce_scatter | solution.py:54
  894.1 125.4 %reduce-scatter.11.cloned.1.call-done = f32[8,256]{1,0:T(8,128)} async-done(((f32[8,8192]{1,0:T(8,128)}), f32[8,256]{1,0:T(8,128)}) %reduce-scatter.11.cloned.1.call-update) | async-done | bytes 8208 | tf_op jit(solution)/shard_map/reduce_scatter | solution.py:57
  1019.5 1.6 convolution_subtract_fusion.1
  1021.2 114.9 %psum.23 = f32[8,8]{0,1:T(8,128)S(1)} all-reduce(f32[8,8]{0,1:T(8,128)S(1)} %fusion.71), channel_id=1, replica_groups=mesh['row'=32,'col'=32] {'row','col'}, use_global_device_ids=true, to_apply=%region_8.10 | all-reduce | flops 64 | bytes 512 | tf_op jit(solution)/shard_map/psum | solution.py:12
  1136.1 0.7 convolution_subtract_fusion
  (56 shorter events, 9.7 us)
Async XLA Ops:
  7.2 52.2 %copy-start = (bf16[1,1,96,128,128]{4,3,2,1,0:T(8,128)(2,1)S(1)}, bf16[1,1,96,128,128]{4,3,2,1,0:T(8,128)(2,1)}, u32[]{:S(2)}) copy-start(bf16[1,1,96,128,128]{4,3,2,1,0:T(8,128)(2,1)} %param.14) | copy-start | bytes 9437188
  7.2 53.9 %copy-start.6 = (s32[1,1,96]{2,1,0:T(1,128)S(1)}, s32[1,1,96]{2,1,0:T(1,128)}, u32[]{:S(2)}) copy-start(s32[1,1,96]{2,1,0:T(1,128)} %param.15) | copy-start | bytes 1156
  7.2 274.7 %reduce-scatter.5.cloned.1.call-start = ((), (), s32[]{:S(2)}) async-start(), calls=%async_computation.4 | async-start | bytes 270336 | tf_op jit(solution)/shard_map/reduce_scatter | solution.py:54
  61.1 71.6 %copy-start.7 = (s32[1,1,96]{2,1,0:T(1,128)S(1)}, s32[1,1,96]{2,1,0:T(1,128)}, u32[]{:S(2)}) copy-start(s32[1,1,96]{2,1,0:T(1,128)} %param.16) | copy-start | bytes 1156
  61.6 346.0 %copy-start.1 = (f32[8,256]{1,0:T(8,128)S(1)}, f32[8,256]{1,0:T(8,128)}, u32[]{:S(2)}) copy-start(f32[8,256]{1,0:T(8,128)} %param.10) | copy-start | bytes 24580
  61.6 346.0 %copy-start.3 = (f32[8,256]{1,0:T(8,128)S(1)}, f32[8,256]{1,0:T(8,128)}, u32[]{:S(2)}) copy-start(f32[8,256]{1,0:T(8,128)} %param.11) | copy-start | bytes 24580
  61.6 345.9 %copy-start.4 = (f32[8,8]{1,0:T(8,128)S(1)}, f32[8,8]{1,0:T(8,128)}, u32[]{:S(2)}) copy-start(f32[8,8]{1,0:T(8,128)} %param.12) | copy-start | bytes 772
  61.6 345.9 %copy-start.5 = (f32[256]{0:T(256)S(1)}, f32[256]{0:T(256)}, u32[]{:S(2)}) copy-start(f32[256]{0:T(256)} %param.13) | copy-start | bytes 3076
  62.5 345.0 %reduce-scatter.7.cloned.1.call-start = ((), (), s32[]{:S(2)}) async-start(), calls=%async_computation.5 | async-start | bytes 270336 | tf_op jit(solution)/shard_map/reduce_scatter | solution.py:57
  134.1 760.0 %reduce-scatter.9.cloned.1.call-start = ((), (), s32[]{:S(2)}) async-start(), calls=%async_computation.6 | async-start | bytes 270336 | tf_op jit(solution)/shard_map/reduce_scatter | solution.py:54
  637.3 498.8 %copy-start.2 = (f32[8,256]{1,0:T(8,128)}, f32[8,256]{1,0:T(8,128)S(1)}, u32[]{:S(2)}) copy-start(f32[8,256]{1,0:T(8,128)S(1)} %get-tuple-element.7) | copy-start | bytes 24580
  674.1 345.4 %reduce-scatter.11.cloned.1.call-start = ((), (), s32[]{:S(2)}) async-start(), calls=%async_computation.7 | async-start | bytes 270336 | tf_op jit(solution)/shard_map/reduce_scatter | solution.py:57
Sparse Core Ops, SparseCore 0:
  62.6 219.2 reduce-scatter.4
  285.7 121.8 reduce-scatter.6
  674.3 219.7 reduce-scatter.8
  897.7 121.8 reduce-scatter.10
where the time goes:
time: 1150 us; the launch traced here: 1140 us
  blocking collectives  556 us (48%)
  waiting for transfers between devices  551 us (48%)
  between operations  14.6 us (1%)
    psum x3, blocking collectives, global_sum(): return lax.psum(values, ('row', 'col'))  340 us
    reduce_scatter x2, waiting for transfers between devices, apply_matrix(): lax.psum_scatter(near_part.reshape(vector_count, -1), 'col', scatter_dime...  300 us
    reduce_scatter x2, waiting for transfers between devices, apply_matrix(): lax.psum_scatter(far_part.reshape(vector_count, -1), 'row', scatter_dimen...  251 us
    all_gather x2, blocking collectives, apply_matrix(): lax.all_gather(rounded, 'col', axis=1, tiled=True)  133 us
    all_gather x2, blocking collectives, apply_matrix(): lax.all_gather(rounded, 'row', axis=1, tiled=True)  81.6 us
  transfers between devices with their start and end apart: 4, of which 4 were waited for; matrix products, arithmetic and copies ran while one was open for 1% of the time, Pallas kernels for 0%

commit v1 on v0

v1 whole, which is shorter than its diff:
```python
import jax
import jax.numpy as jnp
from jax import lax
from jax.sharding import PartitionSpec as P

HIGHEST = lax.Precision.HIGHEST


def exchange(chunks, axis):
    return lax.all_to_all(chunks, axis, split_axis=0, concat_axis=0, tiled=True)


def gather_from(chunk, axis):
    size = lax.axis_size(axis)
    return exchange(jnp.broadcast_to(chunk[None], (size,) + chunk.shape), axis)


def inner(left, right):
    return jnp.einsum("tvi,twi->vw", left, right, precision=HIGHEST)


def mix(matrix, vectors):
    return jnp.einsum("uv,tvi->tui", matrix, vectors, precision=HIGHEST)


def dot(left, right):
    return jnp.dot(left, right, precision=HIGHEST)


def on_device(
    current_block, previous_block, beta_coupling, diagonal, blocks, near_index, far_index, counts
):
    tile_blocks = blocks[0, 0]
    near_list = near_index[0, 0]
    far_list = far_index[0, 0]
    live_count = counts[0, 0]
    nv, share = current_block.shape
    width = tile_blocks.shape[-1]
    pb = share // width
    slots = tile_blocks.shape[0]
    n_row, n_col = lax.axis_size("row"), lax.axis_size("col")
    rows_total = share * n_row * n_col
    live_mask = (jnp.arange(slots) < live_count).astype(jnp.float32)
    near_total, far_total = n_col * pb, n_row * pb
    pick_near = (near_list[:, None] == jnp.arange(near_total)[None, :]).astype(
        jnp.float32
    ) * live_mask[:, None]
    pick_far = (far_list[:, None] == jnp.arange(far_total)[None, :]).astype(
        jnp.float32
    ) * live_mask[:, None]

    def local_form(vectors):
        return vectors.reshape(nv, pb, width).transpose(1, 0, 2)

    def tile_products(near_vectors, far_vectors):
        from_far = jnp.take(far_vectors, far_list, axis=0)
        from_near = jnp.take(near_vectors, near_list, axis=0)
        to_near = jnp.einsum(
            "kvj,kij->kvi", from_far, tile_blocks, preferred_element_type=jnp.float32
        )
        to_far = jnp.einsum(
            "kvi,kij->kvj", from_near, tile_blocks, preferred_element_type=jnp.float32
        )
        return to_near, to_far

    def place(products, pick):
        return jnp.einsum("kvi,kn->nvi", products, pick, precision=HIGHEST)

    current = local_form(current_block)
    previous = local_form(previous_block)
    diag = diagonal.reshape(pb, 1, width)

    rounded = current.astype(jnp.bfloat16).reshape(pb * nv, width)
    near_vectors = gather_from(rounded, "col").reshape(near_total, nv, width)
    far_vectors = gather_from(rounded, "row").reshape(far_total, nv, width)
    to_near, to_far = tile_products(near_vectors, far_vectors)
    near_part = place(to_near, pick_near).reshape(n_col, pb, nv, width)
    far_part = place(to_far, pick_far).reshape(n_row, pb, nv, width)
    off_diagonal = exchange(near_part, "col").sum(0) + exchange(far_part, "row").sum(0)
    applied = off_diagonal + diag * current
    product = applied - mix(beta_coupling, previous)

    grams = jnp.concatenate(
        [
            inner(current, product),
            inner(product, product),
            inner(current, current),
            inner(product, applied),
            inner(current, applied),
        ],
        axis=1,
    )
    grams = jnp.pad(grams, ((0, 0), (0, width - grams.shape[1])))
    got = gather_from(jnp.concatenate([product, grams[None]]), "col")
    grams = got[:, pb].sum(0)
    near_product = got[:, :pb].reshape(near_total, nv, width)
    got = gather_from(jnp.concatenate([product, grams[None]]), "row")
    grams = got[:, pb].sum(0)
    far_product = got[:, :pb].reshape(far_total, nv, width)

    def split(vectors):
        high = vectors.astype(jnp.bfloat16)
        low = (vectors - high.astype(jnp.float32)).astype(jnp.bfloat16)
        return jnp.concatenate([high, low], axis=1)

    to_near, to_far = tile_products(split(near_product), split(far_product))
    to_near = to_near[:, :nv] + to_near[:, nv:]
    to_far = to_far[:, :nv] + to_far[:, nv:]
    near_part = place(to_near, pick_near)
    far_part = place(to_far, pick_far).reshape(n_row, pb, nv, width)
    quadratic = inner(near_product, near_part)
    quadratic = quadratic + quadratic.T + inner(product, diag * product)
    quadratic = jnp.pad(quadratic, ((0, 0), (0, width - nv)))
    near_part = jnp.concatenate(
        [
            near_part.reshape(n_col, pb, nv, width),
            jnp.broadcast_to(quadratic, (n_col, 1, nv, width)),
        ],
        axis=1,
    )
    near_got = exchange(near_part, "col").sum(0)
    far_part = jnp.concatenate(
        [far_part, jnp.broadcast_to(near_got[pb], (n_row, 1, nv, width))], axis=1
    )
    far_got = exchange(far_part, "row").sum(0)
    applied_product = near_got[:pb] + far_got[:pb] + diag * product
    pw = far_got[pb, :, :nv]

    cp, pp, cc, pu, cu = (grams[:, i * nv : (i + 1) * nv] for i in range(5))
    alpha_one = cp / rows_total
    at = alpha_one.T
    moment = (pp - dot(at, cp) - dot(cp.T, alpha_one) + dot(dot(at, cc), alpha_one)) / rows_total
    factor = jnp.linalg.cholesky(moment)
    inverse = lax.linalg.triangular_solve(
        factor, jnp.eye(nv, dtype=jnp.float32), left_side=True, lower=True
    )
    next_block = mix(inverse, product - mix(at, current))
    second = mix(inverse, applied_product - mix(at, applied)) - mix(factor.T, current)
    half = dot(pu, alpha_one)
    vhv = dot(dot(inverse, pw - half - half.T + dot(dot(at, cu), alpha_one)), inverse.T)
    vc = dot(inverse, cp.T - dot(at, cc))
    alpha_two = (vhv - dot(vc, factor)) / rows_total
    residual = second - mix(alpha_two.T, next_block)

    def whole_form(vectors):
        return vectors.transpose(1, 0, 2).reshape(nv, share)

    return (
        whole_form(residual),
        whole_form(next_block),
        jnp.stack([alpha_one, factor, alpha_two]),
    )


def solution(mesh):
    return jax.shard_map(
        on_device,
        mesh=mesh,
        in_specs=(
            P(None, ("row", "col")),
            P(None, ("row", "col")),
            P(),
            P(("row", "col")),
            P("row", "col", None, None, None),
            P("row", "col", None),
            P("row", "col", None),
            P("row", "col"),
        ),
        out_specs=(P(None, ("row", "col")), P(None, ("row", "col")), P()),
        check_vma=False,
    )
```

time: 1150 us -> 201 us (0.17)
  blocking collectives: 556 us -> 19.3 us
  waiting for transfers between devices: 551 us -> 40.7 us
  starting transfers between devices: 0.16 us -> 61.8 us
  other arithmetic: 5.59 us -> 24.2 us
  local copies, waits for them, and re-layouts: 6.32 us -> 23.3 us
  matrix products: 11.1 us -> 27.4 us
  between operations: 14.6 us -> 1.61 us
    reduce_scatter x4 -> x0, waiting for transfers between devices: 551 us -> none  [the longest x2 300 us: apply_matrix(): lax.psum_scatter(near_part.reshape(vector_count, -1), 'col', scatter_dime...]
    psum x3 -> x0, blocking collectives: 340 us -> none  [global_sum(): return lax.psum(values, ('row', 'col'))]
    all_gather x4 -> x0, blocking collectives: 215 us -> none  [the longest x2 133 us: apply_matrix(): lax.all_gather(rounded, 'col', axis=1, tiled=True)]
    all_to_all x0 -> x7, starting transfers between devices: none -> 61.8 us  [exchange(): return lax.all_to_all(chunks, axis, split_axis=0, concat_axis=0, tiled=True)]
    all_to_all x0 -> x7, waiting for transfers between devices: none -> 40.7 us  [exchange(): return lax.all_to_all(chunks, axis, split_axis=0, concat_axis=0, tiled=True)]
    all_to_all x0 -> x1, blocking collectives: none -> 19.3 us  [exchange(): return lax.all_to_all(chunks, axis, split_axis=0, concat_axis=0, tiled=True)]
    dot_general x15 -> x33, matrix products: 10.9 us -> 26.5 us  [the longest x11 7.6 us: dot(): return jnp.dot(left, right, precision=HIGHEST)]
  transfers between devices with their start and end apart: 4 -> 7, of which waited for: 4 -> 6; matrix products, arithmetic and copies ran while one was open for 1% -> 23% of each run, Pallas kernels for 0% -> 0%
where the time goes in v1:
time: 201 us; the launch traced here: 198 us
  starting transfers between devices  61.8 us (31%)
  waiting for transfers between devices  40.7 us (20%)
  matrix products  27.4 us (14%)
  other arithmetic  24.2 us (12%)
  local copies, waits for them, and re-layouts  23.3 us (12%)
  blocking collectives  19.3 us (10%)
    all_to_all x7, starting transfers between devices, exchange(): return lax.all_to_all(chunks, axis, split_axis=0, concat_axis=0, tiled=True)  61.8 us
    all_to_all x7, waiting for transfers between devices, exchange(): return lax.all_to_all(chunks, axis, split_axis=0, concat_axis=0, tiled=True)  40.7 us
    all_to_all x1, blocking collectives, exchange(): return lax.all_to_all(chunks, axis, split_axis=0, concat_axis=0, tiled=True)  19.3 us
    dot_general x11, matrix products, dot(): return jnp.dot(left, right, precision=HIGHEST)  7.6 us
    dot_general x7, matrix products, mix(): return jnp.einsum('uv,tvi->tui', matrix, vectors, precision=HIGHEST)  5.64 us
    dot_general x2, matrix products, tile_products(): jnp.einsum('kvj,kij->kvi', from_far, tile_blocks, preferred_element_type=...  5.47 us
    gather x2, local copies, waits for them, and re-layouts, tile_products(): from_far = jnp.take(far_vectors, far_list, axis=0)  4.07 us
  transfers between devices with their start and end apart: 7, of which 6 were waited for; matrix products, arithmetic and copies ran while one was open for 23% of the time, Pallas kernels for 0%

profile of v1, /device:TPU:1, one launch (start us, length us, event | category | flops | bytes accessed | tf_op | source)
XLA Modules:
  0.0 198.2 jit_solution(13157557973417747034)
XLA Ops:
  2.2 13.4 %all-to-all-start.2 = ((bf16[32,16,128]{2,1,0:T(8,128)(2,1)}), bf16[32,16,128]{2,1,0:T(8,128)(2,1)S(1)}, u32[]{:S(2)}, u32[]{:S(2)}) async-start(bf16[32,16,128]{2,1,0:T(8,128)(2,1)} %broadcast_in_dim.59), calls=%async_computation.2 | async-start | bytes 262144 | tf_op jit(solution)/shard_map/all_to_all | solution.py:10
  20.1 6.7 %all-to-all-done.2 = bf16[32,16,128]{2,1,0:T(8,128)(2,1)S(1)} async-done(((bf16[32,16,128]{2,1,0:T(8,128)(2,1)}), bf16[32,16,128]{2,1,0:T(8,128)(2,1)S(1)}, u32[]{:S(2)}, u32[]{:S(2)}) %all-to-all-start.2) | async-done | bytes 131104 | tf_op jit(solution)/shard_map/all_to_all | solution.py:10
  26.8 19.0 %all-to-all-start = ((bf16[32,16,128]{2,1,0:T(8,128)(2,1)}), bf16[32,16,128]{2,1,0:T(8,128)(2,1)S(1)}, u32[]{:S(2)}, u32[]{:S(2)}) async-start(bf16[32,16,128]{2,1,0:T(8,128)(2,1)} %broadcast_in_dim.59), calls=%async_computation | async-start | bytes 262144 | tf_op jit(solution)/shard_map/all_to_all | solution.py:10
  47.2 1.9 fusion.4
  50.3 4.0 %all-to-all-done = bf16[32,16,128]{2,1,0:T(8,128)(2,1)S(1)} async-done(((bf16[32,16,128]{2,1,0:T(8,128)(2,1)}), bf16[32,16,128]{2,1,0:T(8,128)(2,1)S(1)}, u32[]{:S(2)}, u32[]{:S(2)}) %all-to-all-start) | async-done | bytes 131104 | tf_op jit(solution)/shard_map/all_to_all | solution.py:10
  54.3 4.9 %all-to-all-start.3 = ((f32[32,2,8,128]{3,1,2,0:T(2,128)}), f32[32,2,8,128]{3,1,2,0:T(2,128)S(1)}, u32[]{:S(2)}, u32[]{:S(2)}) async-start(f32[32,2,8,128]{3,1,2,0:T(2,128)} %copy.59), calls=%async_computation.3 | async-start | bytes 524288 | tf_op jit(solution)/shard_map/all_to_all | solution.py:10
  60.8 2.7 %fusion.6 = f32[96,8,128]{2,1,0:T(8,128)S(1)} fusion(bf16[1,1,96,128,128]{4,3,2,1,0:T(8,128)(2,1)S(1)} %copy-done, bf16[96,8,128]{2,1,0:T(8,128)(2,1)} %gather_fusion, pred[96]{0:T(512)(128)(4,1)} %compare_and_fusion.1), kind=kOutput, calls=%fused_computation.10 | convolution fusion | flops 25264128 | bytes 3735648 | tf_op jit(solution)/shard_map/kvj,kij->kvi/dot_general | solution.py:58
  65.5 4.8 %all-to-all-done.3 = f32[32,2,8,128]{3,1,2,0:T(2,128)S(1)} async-done(((f32[32,2,8,128]{3,1,2,0:T(2,128)}), f32[32,2,8,128]{3,1,2,0:T(2,128)S(1)}, u32[]{:S(2)}, u32[]{:S(2)}) %all-to-all-start.3) | async-done | bytes 262176 | tf_op jit(solution)/shard_map/all_to_all | solution.py:10
  70.3 4.6 %all-to-all-start.1 = ((f32[32,2,8,128]{3,1,2,0:T(2,128)}), f32[32,2,8,128]{3,1,2,0:T(2,128)}, u32[]{:S(2)}, u32[]{:S(2)}) async-start(f32[32,2,8,128]{3,1,2,0:T(2,128)} %copy.56), calls=%async_computation.1 | async-start | bytes 524288 | tf_op jit(solution)/shard_map/all_to_all | solution.py:10
  75.1 11.4 %all-to-all-done.1 = f32[32,2,8,128]{3,1,2,0:T(2,128)} async-done(((f32[32,2,8,128]{3,1,2,0:T(2,128)}), f32[32,2,8,128]{3,1,2,0:T(2,128)}, u32[]{:S(2)}, u32[]{:S(2)}) %all-to-all-start.1) | async-done | bytes 262176 | tf_op jit(solution)/shard_map/all_to_all | solution.py:10
  88.5 19.3 %all_to_all.40 = f32[32,3,8,128]{3,2,1,0:T(8,128)S(1)} all-to-all(f32[32,3,8,128]{3,2,1,0:T(8,128)S(1)} %broadcast_in_dim.61), channel_id=1, replica_groups=mesh['row'=32,'col'=32] {'col'}, dimensions={0} | all-to-all | bytes 786432 | tf_op jit(solution)/shard_map/all_to_all | solution.py:10
  109.3 9.7 %all-to-all-start.5 = ((f32[32,3,8,128]{3,2,1,0:T(8,128)}), f32[32,3,8,128]{3,2,1,0:T(8,128)}, u32[]{:S(2)}, u32[]{:S(2)}) async-start(f32[32,3,8,128]{3,2,1,0:T(8,128)} %broadcast_in_dim.63), calls=%async_computation.5 | async-start | bytes 786432 | tf_op jit(solution)/shard_map/all_to_all | solution.py:10
  120.7 2.5 %gather_fusion.3 = bf16[96,16,128]{2,1,0:T(8,128)(2,1)} fusion(bf16[64,16,128]{2,1,0:T(8,128)(2,1)} %pad_maximum_fusion.3, s32[1024]{0:T(1024)} %copy-done.10), kind=kCustom, calls=%fused_computation.3.clone | custom fusion | bytes 786816 | tf_op jit(solution)/shard_map/jit(_take)/gather | solution.py:57
  123.2 2.0 fusion
  126.5 6.4 %all-to-all-done.5 = f32[32,3,8,128]{3,2,1,0:T(8,128)} async-done(((f32[32,3,8,128]{3,2,1,0:T(8,128)}), f32[32,3,8,128]{3,2,1,0:T(8,128)}, u32[]{:S(2)}, u32[]{:S(2)}) %all-to-all-start.5) | async-done | bytes 393248 | tf_op jit(solution)/shard_map/all_to_all | solution.py:10
  134.7 2.5 %gather_fusion.2 = bf16[96,16,128]{2,1,0:T(8,128)(2,1)} fusion(bf16[64,16,128]{2,1,0:T(8,128)(2,1)} %pad_maximum_fusion.2, s32[1024]{0:T(1024)} %pad_clamp_fusion.1), kind=kCustom, calls=%fused_computation.1.clone | custom fusion | bytes 786816 | tf_op jit(solution)/shard_map/jit(_take)/gather | solution.py:56
  137.2 2.8 %fusion.2 = f32[96,16,128]{2,1,0:T(8,128)S(1)} fusion(bf16[1,1,96,128,128]{4,3,2,1,0:T(8,128)(2,1)S(1)} %copy-done, bf16[96,16,128]{2,1,0:T(8,128)(2,1)} %gather_fusion.2, pred[96]{0:T(512)(128)(4,1)S(1)} %copy-done.15), kind=kOutput, calls=%fused_computation.6 | convolution fusion | flops 50528256 | bytes 4325472 | tf_op jit(solution)/shard_map/kvj,kij->kvi/dot_general | solution.py:58
  144.0 4.7 %all-to-all-start.6 = ((f32[32,3,8,128]{3,2,1,0:T(8,128)}), f32[32,3,8,128]{3,2,1,0:T(8,128)S(1)}, u32[]{:S(2)}, u32[]{:S(2)}) async-start(f32[32,3,8,128]{3,2,1,0:T(8,128)} %pad_maximum_fusion), calls=%async_computation.6 | async-start | bytes 786432 | tf_op jit(solution)/shard_map/all_to_all | solution.py:10
  157.0 2.0 %cholesky.17 = f32[8,8]{1,0:T(8,128)} custom-call(f32[8,8]{1,0:T(8,128)} %fusion.78), custom_call_target="Cholesky" | custom-call | tf_op jit(solution)/shard_map/jit(cholesky)/cholesky | solution.py:133
  160.4 1.9 fusion.87
  162.3 1.9 custom-call.6
  167.7 1.7 pad_maximum_fusion.1
  169.5 5.4 %all-to-all-start.7 = ((f32[32,3,8,128]{3,2,1,0:T(8,128)}), f32[32,3,8,128]{3,2,1,0:T(8,128)S(1)}, u32[]{:S(2)}, u32[]{:S(2)}) async-start(f32[32,3,8,128]{3,2,1,0:T(8,128)} %pad_maximum_fusion.1), calls=%async_computation.7 | async-start | bytes 786432 | tf_op jit(solution)/shard_map/all_to_all | solution.py:10
  181.4 7.4 %all-to-all-done.7 = f32[32,3,8,128]{3,2,1,0:T(8,128)S(1)} async-done(((f32[32,3,8,128]{3,2,1,0:T(8,128)}), f32[32,3,8,128]{3,2,1,0:T(8,128)S(1)}, u32[]{:S(2)}, u32[]{:S(2)}) %all-to-all-start.7) | async-done | bytes 393248 | tf_op jit(solution)/shard_map/all_to_all | solution.py:10
  (122 shorter events, 53.0 us)
Async XLA Ops:
  0.6 46.5 %copy-start = (bf16[1,1,96,128,128]{4,3,2,1,0:T(8,128)(2,1)S(1)}, bf16[1,1,96,128,128]{4,3,2,1,0:T(8,128)(2,1)}, u32[]{:S(2)}) copy-start(bf16[1,1,96,128,128]{4,3,2,1,0:T(8,128)(2,1)} %param.16) | copy-start | bytes 9437188
  0.6 48.4 %copy-start.12 = (s32[1,1,96]{2,1,0:T(1,128)S(1)}, s32[1,1,96]{2,1,0:T(1,128)}, u32[]{:S(2)}) copy-start(s32[1,1,96]{2,1,0:T(1,128)} %param.18) | copy-start | bytes 1156
  2.2 24.7 %all-to-all-start.2 = ((bf16[32,16,128]{2,1,0:T(8,128)(2,1)}), bf16[32,16,128]{2,1,0:T(8,128)(2,1)S(1)}, u32[]{:S(2)}, u32[]{:S(2)}) async-start(bf16[32,16,128]{2,1,0:T(8,128)(2,1)} %broadcast_in_dim.59), calls=%async_computation.2 | async-start | bytes 262144 | tf_op jit(solution)/shard_map/all_to_all | solution.py:10
  16.9 37.4 %copy-start.16 = (pred[96]{0:T(512)(128)(4,1)}, pred[96]{0:T(512)(128)(4,1)S(1)}, u32[]{:S(2)}) copy-start(pred[96]{0:T(512)(128)(4,1)S(1)} %compare_and_fusion) | copy-start | bytes 292
  16.9 42.3 %copy-start.10 = (s32[1024]{0:T(1024)}, s32[1024]{0:T(1024)S(1)}, u32[]{:S(2)}) copy-start(s32[1024]{0:T(1024)S(1)} %pad_clamp_fusion) | copy-start | bytes 12292
  18.9 44.7 %copy-start.7 = (f32[96]{0:T(128)}, f32[96]{0:T(128)S(1)}, u32[]{:S(2)}) copy-start(f32[96]{0:T(128)S(1)} %compare_convert_fusion) | copy-start | bytes 1156
  26.8 27.5 %all-to-all-start = ((bf16[32,16,128]{2,1,0:T(8,128)(2,1)}), bf16[32,16,128]{2,1,0:T(8,128)(2,1)S(1)}, u32[]{:S(2)}, u32[]{:S(2)}) async-start(bf16[32,16,128]{2,1,0:T(8,128)(2,1)} %broadcast_in_dim.59), calls=%async_computation | async-start | bytes 262144 | tf_op jit(solution)/shard_map/all_to_all | solution.py:10
  50.3 24.6 %copy-start.2 = (f32[8,256]{1,0:T(8,128)S(1)}, f32[8,256]{1,0:T(8,128)}, u32[]{:S(2)}) copy-start(f32[8,256]{1,0:T(8,128)} %param.12) | copy-start | bytes 24580
  54.3 16.0 %all-to-all-start.3 = ((f32[32,2,8,128]{3,1,2,0:T(2,128)}), f32[32,2,8,128]{3,1,2,0:T(2,128)S(1)}, u32[]{:S(2)}, u32[]{:S(2)}) async-start(f32[32,2,8,128]{3,1,2,0:T(2,128)} %copy.59), calls=%async_computation.3 | async-start | bytes 524288 | tf_op jit(solution)/shard_map/all_to_all | solution.py:10
  59.2 28.4 %copy-start.5 = (f32[256]{0:T(256)S(1)}, f32[256]{0:T(256)}, u32[]{:S(2)}) copy-start(f32[256]{0:T(256)} %param.15) | copy-start | bytes 3076
  60.8 26.8 %copy-start.9 = (f32[8,256]{1,0:T(8,128)S(1)}, f32[8,256]{1,0:T(8,128)}, u32[]{:S(2)}) copy-start(f32[8,256]{1,0:T(8,128)} %param.13) | copy-start | bytes 24580
  60.8 26.8 %copy-start.11 = (f32[8,8]{1,0:T(8,128)S(1)}, f32[8,8]{1,0:T(8,128)}, u32[]{:S(2)}) copy-start(f32[8,8]{1,0:T(8,128)} %param.14) | copy-start | bytes 772
  70.3 16.2 %all-to-all-start.1 = ((f32[32,2,8,128]{3,1,2,0:T(2,128)}), f32[32,2,8,128]{3,1,2,0:T(2,128)}, u32[]{:S(2)}, u32[]{:S(2)}) async-start(f32[32,2,8,128]{3,1,2,0:T(2,128)} %copy.56), calls=%async_computation.1 | async-start | bytes 524288 | tf_op jit(solution)/shard_map/all_to_all | solution.py:10
  87.6 0.6 copy-start.3
  109.3 23.6 %all-to-all-start.5 = ((f32[32,3,8,128]{3,2,1,0:T(8,128)}), f32[32,3,8,128]{3,2,1,0:T(8,128)}, u32[]{:S(2)}, u32[]{:S(2)}) async-start(f32[32,3,8,128]{3,2,1,0:T(8,128)} %broadcast_in_dim.63), calls=%async_computation.5 | async-start | bytes 786432 | tf_op jit(solution)/shard_map/all_to_all | solution.py:10
  120.7 4.5 %copy-start.8 = (f32[96]{0:T(128)S(1)}, f32[96]{0:T(128)}, u32[]{:S(2)}) copy-start(f32[96]{0:T(128)} %copy-done.7) | copy-start | bytes 1156
  120.7 4.5 %copy-start.13 = (s32[1,1,96]{2,1,0:T(1,128)S(1)}, s32[1,1,96]{2,1,0:T(1,128)}, u32[]{:S(2)}) copy-start(s32[1,1,96]{2,1,0:T(1,128)} %param.18) | copy-start | bytes 1156
  125.2 12.0 %copy-start.15 = (pred[96]{0:T(512)(128)(4,1)S(1)}, pred[96]{0:T(512)(128)(4,1)}, u32[]{:S(2)}) copy-start(pred[96]{0:T(512)(128)(4,1)} %compare_and_fusion.1) | copy-start | bytes 292
  134.7 5.3 %copy-start.14 = (s32[1,1,96]{2,1,0:T(1,128)S(1)}, s32[1,1,96]{2,1,0:T(1,128)}, u32[]{:S(2)}) copy-start(s32[1,1,96]{2,1,0:T(1,128)} %param.17) | copy-start | bytes 1156
  137.2 4.8 %copy-start.6 = (f32[256]{0:T(256)S(1)}, f32[256]{0:T(256)}, u32[]{:S(2)}) copy-start(f32[256]{0:T(256)} %param.15) | copy-start | bytes 3076
  140.5 0.7 copy-start.1
  144.0 22.4 %all-to-all-start.6 = ((f32[32,3,8,128]{3,2,1,0:T(8,128)}), f32[32,3,8,128]{3,2,1,0:T(8,128)S(1)}, u32[]{:S(2)}, u32[]{:S(2)}) async-start(f32[32,3,8,128]{3,2,1,0:T(8,128)} %pad_maximum_fusion), calls=%async_computation.6 | async-start | bytes 786432 | tf_op jit(solution)/shard_map/all_to_all | solution.py:10
  152.6 1.0 copy-start.4
  169.5 19.3 %all-to-all-start.7 = ((f32[32,3,8,128]{3,2,1,0:T(8,128)}), f32[32,3,8,128]{3,2,1,0:T(8,128)S(1)}, u32[]{:S(2)}, u32[]{:S(2)}) async-start(f32[32,3,8,128]{3,2,1,0:T(8,128)} %pad_maximum_fusion.1), calls=%async_computation.7 | async-start | bytes 786432 | tf_op jit(solution)/shard_map/all_to_all | solution.py:10

commit v2 on v0

v2 whole, which is shorter than its diff:
```python
import functools

import jax
import jax.numpy as jnp
from jax import lax
from jax.experimental import pallas as pl
from jax.experimental.pallas import tpu as pltpu
from jax.sharding import PartitionSpec as P

HIGHEST = lax.Precision.HIGHEST
F32 = jnp.float32
BF16 = jnp.bfloat16
SHIFT = 1.25
VMEM = pl.BlockSpec(memory_space=pltpu.VMEM)
SMEM = pl.BlockSpec(memory_space=pltpu.SMEM)
PARAMS = pltpu.CompilerParams(vmem_limit_bytes=24 * 1024 * 1024)


def exchange(chunks, axis):
    return lax.all_to_all(chunks, axis, split_axis=0, concat_axis=0, tiled=True)


def call(kernel, out_shape, in_specs, scratch=()):
    many = isinstance(out_shape, (list, tuple))
    return pl.pallas_call(
        kernel,
        out_shape=out_shape,
        in_specs=in_specs,
        out_specs=tuple(VMEM for _ in out_shape) if many else VMEM,
        scratch_shapes=list(scratch),
        compiler_params=PARAMS,
    )


def shape_of(shape, dtype=F32):
    return jax.ShapeDtypeStruct(shape, dtype)


def pieces(ref):
    width = ref.shape[-1] // 2
    return [ref[:, :width], ref[:, width:]]


def contract_last(left, right):
    return lax.dot_general(
        left, right, (((1,), (1,)), ((), ())), precision=HIGHEST, preferred_element_type=F32
    )


def small_dot(left, right):
    total = left[:, 0:1] * right[0:1, :]
    for k in range(1, right.shape[0]):
        total = total + left[:, k : k + 1] * right[k : k + 1, :]
    return total


def identity(size):
    rows = lax.broadcasted_iota(jnp.int32, (size, size), 0)
    return (rows == lax.broadcasted_iota(jnp.int32, (size, size), 1)).astype(F32)


def rounded_kernel(vectors_ref, out_ref):
    chunk = jnp.concatenate(pieces(vectors_ref), axis=0).astype(BF16)
    out_ref[...] = jnp.broadcast_to(chunk[None], out_ref.shape)


def multiply_slots(src_ref, vectors_ref, blocks_ref, products_ref, over_columns):
    dims = (((1,), (1 if over_columns else 0,)), ((), ()))
    for k in range(blocks_ref.shape[0]):
        pair = vectors_ref[lax.shift_right_logical(src_ref[k], 1)]
        products_ref[k] = lax.dot_general(
            pair, blocks_ref[k], dims, preferred_element_type=F32
        )


def place_slots(src_ref, dst_ref, count_ref, products_ref, add):
    nv = products_ref.shape[1] // 2

    def one_slot(k, carry):
        half = pl.multiple_of((src_ref[k] & 1) * nv, nv)
        add(dst_ref[k], products_ref[k, pl.ds(half, nv), :])
        return carry

    lax.fori_loop(0, count_ref[0], one_slot, 0)


def products_kernel(
    over_columns, src_ref, dst_ref, count_ref, vectors_ref, blocks_ref, out_ref, products_ref
):
    multiply_slots(src_ref, vectors_ref, blocks_ref, products_ref, over_columns)
    out_ref[...] = jnp.zeros_like(out_ref)

    def add(block, values):
        out_ref[block >> 1, block & 1] += values

    place_slots(src_ref, dst_ref, count_ref, products_ref, add)


def near_kernel(
    src_ref,
    dst_ref,
    count_ref,
    vectors_ref,
    near_ref,
    blocks_ref,
    shifted_ref,
    diagonal_ref,
    grams_ref,
    out_ref,
    products_ref,
):
    products_kernel(
        True, src_ref, dst_ref, count_ref, vectors_ref, blocks_ref, out_ref, products_ref
    )
    nv, width = out_ref.shape[2:]
    total = jnp.zeros((2 * nv, 2 * nv), F32)
    for n in range(out_ref.shape[0]):
        pair = jnp.concatenate([out_ref[n, 0], out_ref[n, 1]], axis=0)
        total = total + contract_last(pair, near_ref[n].astype(F32))
    quadratic = total[:nv, :nv] + total[nv:, nv:]
    quadratic = quadratic + contract_last(identity(nv), quadratic)
    for vectors, diag in zip(pieces(shifted_ref), pieces(diagonal_ref)):
        quadratic = quadratic + contract_last(vectors, diag * vectors)
    used = 9 * nv
    extra = jnp.concatenate(
        [grams_ref[:, :used], quadratic, jnp.zeros((nv, width - used - nv), F32)], axis=1
    )
    for n in range(out_ref.shape[0]):
        out_ref[n, 2] = extra


def middle_kernel(
    near_ref,
    far_ref,
    current_ref,
    previous_ref,
    beta_ref,
    diagonal_ref,
    applied_ref,
    shifted_ref,
    payload_ref,
    grams_ref,
):
    nv, width = near_ref.shape[2:]
    beta = beta_ref[...]
    total = jnp.zeros((3 * nv, 3 * nv), F32)
    halves = []
    for t in range(2):
        part = slice(t * width, (t + 1) * width)
        current = current_ref[:, part]
        off_diagonal = jnp.sum(near_ref[:, t], axis=0) + jnp.sum(far_ref[:, t], axis=0)
        applied = off_diagonal + diagonal_ref[:, part] * current
        shifted = applied - small_dot(beta, previous_ref[:, part]) - SHIFT * current
        applied_ref[:, part] = applied
        shifted_ref[:, part] = shifted
        stack = jnp.concatenate([current, shifted, applied], axis=0)
        total = total + contract_last(stack, stack)
        halves.append(shifted)
    chunk = jnp.concatenate(halves, axis=0).astype(BF16)
    payload_ref[...] = jnp.broadcast_to(chunk[None], payload_ref.shape)
    grams_ref[...] = jnp.concatenate(
        [total[:nv], total[nv : 2 * nv], total[2 * nv :], jnp.zeros((nv, width - 9 * nv), F32)],
        axis=1,
    )


def forward_kernel(near_ref, far_ref, sum_ref, out_ref):
    total = jnp.sum(near_ref[...], axis=0)
    sum_ref[...] = total[:2]
    out_ref[:, :2] = far_ref[...]
    out_ref[:, 2] = jnp.broadcast_to(total[2][None], out_ref[:, 2].shape)


def last_kernel(
    rows_total,
    near_ref,
    far_ref,
    current_ref,
    shifted_ref,
    applied_ref,
    diagonal_ref,
    residual_ref,
    next_ref,
    coefficients_ref,
):
    nv, width = near_ref.shape[1:]
    received = jnp.sum(far_ref[...], axis=0)
    extra = received[2]
    gram = lambda i: extra[:, i * nv : (i + 1) * nv]
    cc, cx, cu, xc, xx, xu, _, ux, _, xw = (gram(i) for i in range(10))
    eye = identity(nv)
    scale = 1.0 / rows_total
    alpha_one = (cx + SHIFT * cc) * scale
    alpha = alpha_one - SHIFT * eye
    alpha_t = (xc + SHIFT * cc) * scale - SHIFT * eye
    adjusted_c = xc - small_dot(alpha_t, cc)
    work = (xx - small_dot(alpha_t, cx) - small_dot(adjusted_c, alpha)) * scale
    rows = lax.broadcasted_iota(jnp.int32, (nv, nv), 0)
    columns = lax.broadcasted_iota(jnp.int32, (nv, nv), 1)
    factor = jnp.zeros((nv, nv), F32)
    factor_t = jnp.zeros((nv, nv), F32)
    inverse = eye
    for j in range(nv):
        root = lax.rsqrt(work[j : j + 1, j : j + 1])
        column = jnp.where(rows[:, :1] >= j, work[:, j : j + 1] * root, 0.0)
        row = jnp.where(columns[:1] >= j, work[j : j + 1, :] * root, 0.0)
        factor = jnp.where(columns == j, column, factor)
        factor_t = jnp.where(rows == j, row, factor_t)
        work = work - column * row
        done = inverse[j : j + 1, :] * root
        below = jnp.where(rows[:, :1] > j, column, 0.0)
        inverse = jnp.where(rows == j, done, inverse - below * done)
    z = (
        xw
        - small_dot(xu, alpha)
        - small_dot(alpha_t, ux)
        + small_dot(small_dot(alpha_t, cu), alpha)
    )
    alpha_two = contract_last(small_dot(inverse, z), inverse)
    alpha_two = (alpha_two - small_dot(small_dot(inverse, adjusted_c), factor)) * scale
    alpha_two_t = contract_last(eye, alpha_two)
    for t in range(2):
        part = slice(t * width, (t + 1) * width)
        current = current_ref[:, part]
        shifted = shifted_ref[:, part]
        applied_shifted = near_ref[t] + received[t] + diagonal_ref[:, part] * shifted
        following = small_dot(inverse, shifted - small_dot(alpha_t, current))
        second = small_dot(inverse, applied_shifted - small_dot(alpha_t, applied_ref[:, part]))
        second = second - small_dot(factor_t, current)
        next_ref[:, part] = following
        residual_ref[:, part] = second - small_dot(alpha_two_t, following)
    coefficients_ref[0] = alpha_one
    coefficients_ref[1] = factor
    coefficients_ref[2] = alpha_two


def on_device(
    current_block, previous_block, beta_coupling, diagonal, blocks, near_index, far_index, counts
):
    tile_blocks = blocks[0, 0]
    near_list = near_index[0, 0]
    far_list = far_index[0, 0]
    live_count = counts[0]
    nv, share = current_block.shape
    slots, width = tile_blocks.shape[:2]
    n_row, n_col = lax.axis_size("row"), lax.axis_size("col")
    rows_total = share * n_row * n_col
    diag = diagonal.reshape(1, share)
    vector = shape_of((nv, share))

    def products(over_columns, src, dst, vectors, peers):
        return call(
            functools.partial(products_kernel, over_columns),
            shape_of((peers, 2, nv, width)),
            [SMEM] * 3 + [VMEM] * 2,
            [pltpu.VMEM((slots, 2 * nv, width), F32)],
        )(src, dst, live_count, vectors, tile_blocks)

    chunks = call(rounded_kernel, shape_of((n_col, 2 * nv, width), BF16), [VMEM])(current_block)
    near_vectors = exchange(chunks, "col")
    far_vectors = exchange(chunks, "row")
    far_part = products(False, near_list, far_list, near_vectors, n_row)
    far_got = exchange(far_part, "row")
    near_part = products(True, far_list, near_list, far_vectors, n_col)
    near_got = exchange(near_part, "col")
    applied, shifted, chunks, grams = call(
        middle_kernel,
        (vector, vector, shape_of((n_col, 2 * nv, width), BF16), shape_of((nv, width))),
        [VMEM] * 6,
    )(near_got, far_got, current_block, previous_block, beta_coupling, diag)

    far_vectors = exchange(chunks, "row")
    near_vectors = exchange(chunks, "col")
    near_part = call(
        near_kernel,
        shape_of((n_col, 3, nv, width)),
        [SMEM] * 3 + [VMEM] * 6,
        [pltpu.VMEM((slots, 2 * nv, width), F32)],
    )(
        far_list,
        near_list,
        live_count,
        far_vectors,
        near_vectors,
        tile_blocks,
        shifted,
        diag,
        grams,
    )
    near_got = exchange(near_part, "col")
    far_part = products(False, near_list, far_list, near_vectors, n_row)
    near_sum, far_part = call(
        forward_kernel, (shape_of((2, nv, width)), shape_of((n_row, 3, nv, width))), [VMEM] * 2
    )(near_got, far_part)
    far_got = exchange(far_part, "row")
    return call(
        functools.partial(last_kernel, rows_total),
        (vector, vector, shape_of((3, nv, nv))),
        [VMEM] * 6,
    )(near_sum, far_got, current_block, shifted, applied, diag)


def solution(mesh):
    return jax.shard_map(
        on_device,
        mesh=mesh,
        in_specs=(
            P(None, ("row", "col")),
            P(None, ("row", "col")),
            P(),
            P(("row", "col")),
            P("row", "col", None, None, None),
            P("row", "col", None),
            P("row", "col", None),
            P("row", "col"),
        ),
        out_specs=(P(None, ("row", "col")), P(None, ("row", "col")), P()),
        check_vma=False,
    )
```

time: 1150 us -> 177 us (0.15)
  waiting for transfers between devices: 551 us -> 20.1 us
  blocking collectives: 556 us -> 99.1 us
  starting transfers between devices: 0.16 us -> 23.2 us
  Pallas kernels: 0 us -> 16.5 us
  between operations: 14.6 us -> 1.44 us
    reduce_scatter x4 -> x0, waiting for transfers between devices: 551 us -> none  [the longest x2 300 us: apply_matrix(): lax.psum_scatter(near_part.reshape(vector_count, -1), 'col', scatter_dime...]
    psum x3 -> x0, blocking collectives: 340 us -> none  [global_sum(): return lax.psum(values, ('row', 'col'))]
    all_gather x4 -> x0, blocking collectives: 215 us -> none  [the longest x2 133 us: apply_matrix(): lax.all_gather(rounded, 'col', axis=1, tiled=True)]
    all_to_all x0 -> x5, blocking collectives: none -> 99.1 us  [exchange(): return lax.all_to_all(chunks, axis, split_axis=0, concat_axis=0, tiled=True)]
    all_to_all x0 -> x3, starting transfers between devices: none -> 23.2 us  [exchange(): return lax.all_to_all(chunks, axis, split_axis=0, concat_axis=0, tiled=True)]
    all_to_all x0 -> x3, waiting for transfers between devices: none -> 20.1 us  [exchange(): return lax.all_to_all(chunks, axis, split_axis=0, concat_axis=0, tiled=True)]
    pallas_call x0 -> x8, Pallas kernels: none -> 16.5 us  [the longest x3 7.58 us: products(): call(functools.partial(products_kernel, over_columns), shape_of((peers, 2...]
    unnamed x20 -> x52, local copies, waits for them, and re-layouts: 3.45 us -> 15.3 us
  transfers between devices with their start and end apart: 4 -> 3, of which waited for: 4 -> 3; matrix products, arithmetic and copies ran while one was open for 1% -> 0% of each run, Pallas kernels for 0% -> 4%
where the time goes in v2:
time: 177 us; the launch traced here: 176 us
  blocking collectives  99.1 us (56%)
  starting transfers between devices  23.2 us (13%)
  waiting for transfers between devices  20.1 us (11%)
  Pallas kernels  16.5 us (9%)
  local copies, waits for them, and re-layouts  15.3 us (9%)
    all_to_all x5, blocking collectives, exchange(): return lax.all_to_all(chunks, axis, split_axis=0, concat_axis=0, tiled=True)  99.1 us
    all_to_all x3, starting transfers between devices, exchange(): return lax.all_to_all(chunks, axis, split_axis=0, concat_axis=0, tiled=True)  23.2 us
    all_to_all x3, waiting for transfers between devices, exchange(): return lax.all_to_all(chunks, axis, split_axis=0, concat_axis=0, tiled=True)  20.1 us
    unnamed x52, local copies, waits for them, and re-layouts  15.3 us
    pallas_call x3, Pallas kernels, products(): call(functools.partial(products_kernel, over_columns), shape_of((peers, 2...  7.58 us
    pallas_call x1, Pallas kernels, on_device(): call(near_kernel, shape_of((n_col, 3, nv, width)), [SMEM] * 3 + [VMEM] *...  4.81 us
  transfers between devices with their start and end apart: 3, of which 3 were waited for; matrix products, arithmetic and copies ran while one was open for 0% of the time, Pallas kernels for 4%

profile of v2, /device:TPU:1, one launch (start us, length us, event | category | flops | bytes accessed | tf_op | source)
XLA Modules:
  0.0 175.6 jit_solution(10041855025052897756)
XLA Ops:
  0.6 0.7 copy-done.9
  2.0 27.7 %all_to_all.40.vectors_ref = bf16[32,16,128]{2,1,0:T(8,128)(2,1)S(1)} all-to-all(bf16[32,16,128]{2,1,0:T(8,128)(2,1)} %shard_map.103), channel_id=1, replica_groups=mesh['row'=32,'col'=32] {'row'}, dimensions={0} | all-to-all | bytes 262144 | tf_op jit(solution)/shard_map/all_to_all | solution.py:20
  29.7 11.7 %all-to-all-start.2 = ((bf16[32,16,128]{2,1,0:T(8,128)(2,1)}), bf16[32,16,128]{2,1,0:T(8,128)(2,1)S(1)}, u32[]{:S(2)}, u32[]{:S(2)}) async-start(bf16[32,16,128]{2,1,0:T(8,128)(2,1)} %shard_map.103), calls=%async_computation.2 | async-start | bytes 262144 | tf_op jit(solution)/shard_map/all_to_all | solution.py:20
  42.1 1.9 %copy-done = bf16[1,1,96,128,128]{4,3,2,1,0:T(8,128)(2,1)S(1)} copy-done((bf16[1,1,96,128,128]{4,3,2,1,0:T(8,128)(2,1)S(1)}, bf16[1,1,96,128,128]{4,3,2,1,0:T(8,128)(2,1)}, u32[]{:S(2)}) %copy-start) | copy-done | bytes 3145752
  45.3 3.1 %shard_map.104 = f32[32,2,8,128]{3,2,1,0:T(8,128)S(1)} custom-call(s32[96]{0:T(128)S(1)} %bitcast.16, s32[96]{0:T(128)S(1)} %bitcast.20, s32[1]{0:T(128)} %bitcast.5.count_ref, bf16[32,16,128]{2,1,0:T(8,128)(2,1)S(1)} %all_to_all.40.vectors_ref, bf16[96,128,128]{2,1,0:T(8,128)(2,1)S(1)} %bitcast.9), custom_call_target="tpu_custom_call" | custom-call | tf_op jit(solution)/shard_map/pallas_call | solution.py:252
  49.0 3.6 %all-to-all-done.2.vectors_ref = bf16[32,16,128]{2,1,0:T(8,128)(2,1)S(1)} async-done(((bf16[32,16,128]{2,1,0:T(8,128)(2,1)}), bf16[32,16,128]{2,1,0:T(8,128)(2,1)S(1)}, u32[]{:S(2)}, u32[]{:S(2)}) %all-to-all-start.2) | async-done | bytes 131104 | tf_op jit(solution)/shard_map/all_to_all | solution.py:20
  52.7 7.6 %all-to-all-start.1 = ((f32[32,2,8,128]{3,2,1,0:T(8,128)}), f32[32,2,8,128]{3,2,1,0:T(8,128)S(1)}, u32[]{:S(2)}, u32[]{:S(2)}) async-start(f32[32,2,8,128]{3,2,1,0:T(8,128)} %copy-done.5), calls=%async_computation.1 | async-start | bytes 524288 | tf_op jit(solution)/shard_map/all_to_all | solution.py:20
  60.3 2.3 %shard_map.105 = f32[32,2,8,128]{3,2,1,0:T(8,128)S(1)} custom-call(s32[96]{0:T(128)S(1)} %bitcast.21, s32[96]{0:T(128)S(1)} %bitcast.17, s32[1]{0:T(128)} %bitcast.6.count_ref, bf16[32,16,128]{2,1,0:T(8,128)(2,1)S(1)} %all-to-all-done.2.vectors_ref, bf16[96,128,128]{2,1,0:T(8,128)(2,1)S(1)} %bitcast.10), custom_call_target="tpu_custom_call" | custom-call | tf_op jit(solution)/shard_map/pallas_call | solution.py:252
  62.6 0.7 copy-done.8
  63.3 8.8 %all-to-all-done.1.near_ref = f32[32,2,8,128]{3,2,1,0:T(8,128)S(1)} async-done(((f32[32,2,8,128]{3,2,1,0:T(8,128)}), f32[32,2,8,128]{3,2,1,0:T(8,128)S(1)}, u32[]{:S(2)}, u32[]{:S(2)}) %all-to-all-start.1) | async-done | bytes 262176 | tf_op jit(solution)/shard_map/all_to_all | solution.py:20
  72.1 19.0 %all_to_all.41.far_ref = f32[32,2,8,128]{3,2,1,0:T(8,128)S(1)} all-to-all(f32[32,2,8,128]{3,2,1,0:T(8,128)} %copy-done.8), channel_id=1, replica_groups=mesh['row'=32,'col'=32] {'row'}, dimensions={0} | all-to-all | bytes 524288 | tf_op jit(solution)/shard_map/all_to_all | solution.py:20
  91.7 0.7 copy-done.14
  93.4 15.2 %all_to_all.42.near_ref.vectors_ref = bf16[32,16,128]{2,1,0:T(8,128)(2,1)S(1)} all-to-all(bf16[32,16,128]{2,1,0:T(8,128)(2,1)S(1)} %get-tuple-element.9), channel_id=1, replica_groups=mesh['row'=32,'col'=32] {'col'}, dimensions={0} | all-to-all | bytes 262144 | tf_op jit(solution)/shard_map/all_to_all | solution.py:20
  108.7 14.2 %all_to_all.43.vectors_ref = bf16[32,16,128]{2,1,0:T(8,128)(2,1)S(1)} all-to-all(bf16[32,16,128]{2,1,0:T(8,128)(2,1)S(1)} %get-tuple-element.9), channel_id=1, replica_groups=mesh['row'=32,'col'=32] {'row'}, dimensions={0} | all-to-all | bytes 262144 | tf_op jit(solution)/shard_map/all_to_all | solution.py:20
  124.9 4.8 %shard_map.107 = f32[32,3,8,128]{3,2,1,0:T(8,128)S(1)} custom-call(s32[96]{0:T(128)S(1)} %bitcast.18, s32[96]{0:T(128)S(1)} %bitcast.22, s32[1]{0:T(128)} %bitcast.7.count_ref, bf16[32,16,128]{2,1,0:T(8,128)(2,1)S(1)} %all_to_all.43.vectors_ref, bf16[32,16,128]{2,1,0:T(8,128)(2,1)S(1)} %all_to_all.42.near_ref.vectors_ref, ...), custom_call_target="tpu_custom_call" | custom-call | tf_op jit(solution)/shard_map/pallas_call | solution.py:274
  129.7 0.7 copy-done.2
  130.5 3.9 %all-to-all-start.6 = ((f32[32,3,8,128]{3,2,1,0:T(8,128)}), f32[32,3,8,128]{3,2,1,0:T(8,128)S(1)}, u32[]{:S(2)}, u32[]{:S(2)}) async-start(f32[32,3,8,128]{3,2,1,0:T(8,128)} %copy-done.2), calls=%async_computation.6 | async-start | bytes 786432 | tf_op jit(solution)/shard_map/all_to_all | solution.py:20
  134.3 0.9 copy-done.4
  136.6 2.3 %shard_map.108.far_ref = f32[32,2,8,128]{3,2,1,0:T(8,128)S(1)} custom-call(s32[96]{0:T(128)S(1)} %bitcast.23, s32[96]{0:T(128)S(1)} %bitcast.19, s32[1]{0:T(128)} %bitcast.8.count_ref, bf16[32,16,128]{2,1,0:T(8,128)(2,1)S(1)} %copy-done.4, bf16[96,128,128]{2,1,0:T(8,128)(2,1)S(1)} %bitcast.12), custom_call_target="tpu_custom_call" | custom-call | tf_op jit(solution)/shard_map/pallas_call | solution.py:252
  139.5 7.7 %all-to-all-done.6.near_ref = f32[32,3,8,128]{3,2,1,0:T(8,128)S(1)} async-done(((f32[32,3,8,128]{3,2,1,0:T(8,128)}), f32[32,3,8,128]{3,2,1,0:T(8,128)S(1)}, u32[]{:S(2)}, u32[]{:S(2)}) %all-to-all-start.6) | async-done | bytes 393248 | tf_op jit(solution)/shard_map/all_to_all | solution.py:20
  147.2 0.9 copy-done.7
  148.2 22.9 %all_to_all.44.far_ref = f32[32,3,8,128]{3,2,1,0:T(8,128)S(1)} all-to-all(f32[32,3,8,128]{3,2,1,0:T(8,128)S(1)} %get-tuple-element.13), channel_id=1, replica_groups=mesh['row'=32,'col'=32] {'row'}, dimensions={0} | all-to-all | bytes 786432 | tf_op jit(solution)/shard_map/all_to_all | solution.py:20
  171.8 0.7 copy-done.24
  172.5 3.1 %shard_map.110 = (f32[8,256]{1,0:T(8,128)}, f32[8,256]{1,0:T(8,128)}, f32[3,8,8]{2,1,0:T(8,128)}) custom-call(f32[2,8,128]{2,1,0:T(8,128)S(1)} %get-tuple-element.12.near_ref, f32[32,3,8,128]{3,2,1,0:T(8,128)S(1)} %all_to_all.44.far_ref, f32[8,256]{1,0:T(8,128)S(1)} %copy-done.10, f32[8,256]{1,0:T(8,128)S(1)} %get-tuple-element.10.shifted_ref, ...), custom_call_target="tpu_custom_call" | custom-call | tf_op jit(solution)/shard_map/pallas_call | solution.py:296
  (47 shorter events, 9.1 us)
Async XLA Ops:
  0.6 0.7 copy-start.9
  1.3 59.0 %copy-start.16 = (s32[1,1,96]{2,1,0:T(1,128)S(1)}, s32[1,1,96]{2,1,0:T(1,128)}, u32[]{:S(2)}) copy-start(s32[1,1,96]{2,1,0:T(1,128)} %param.14) | copy-start | bytes 1156
  1.3 59.0 %copy-start.20 = (s32[1,1,96]{2,1,0:T(1,128)S(1)}, s32[1,1,96]{2,1,0:T(1,128)}, u32[]{:S(2)}) copy-start(s32[1,1,96]{2,1,0:T(1,128)} %param.13) | copy-start | bytes 1156
  29.7 22.9 %all-to-all-start.2 = ((bf16[32,16,128]{2,1,0:T(8,128)(2,1)}), bf16[32,16,128]{2,1,0:T(8,128)(2,1)S(1)}, u32[]{:S(2)}, u32[]{:S(2)}) async-start(bf16[32,16,128]{2,1,0:T(8,128)(2,1)} %shard_map.103), calls=%async_computation.2 | async-start | bytes 262144 | tf_op jit(solution)/shard_map/all_to_all | solution.py:20
  42.1 1.9 %copy-start = (bf16[1,1,96,128,128]{4,3,2,1,0:T(8,128)(2,1)S(1)}, bf16[1,1,96,128,128]{4,3,2,1,0:T(8,128)(2,1)}, u32[]{:S(2)}) copy-start(bf16[1,1,96,128,128]{4,3,2,1,0:T(8,128)(2,1)} %param.12) | copy-start | bytes 9437188
  44.0 0.7 copy-start.15
  45.3 15.0 %copy-start.1 = (bf16[1,1,96,128,128]{4,3,2,1,0:T(8,128)(2,1)S(1)}, bf16[1,1,96,128,128]{4,3,2,1,0:T(8,128)(2,1)}, u32[]{:S(2)}) copy-start(bf16[1,1,96,128,128]{4,3,2,1,0:T(8,128)(2,1)} %param.12) | copy-start | bytes 9437188
  48.4 0.7 copy-start.5
  49.0 42.0 %copy-start.10 = (f32[8,256]{1,0:T(8,128)S(1)}, f32[8,256]{1,0:T(8,128)}, u32[]{:S(2)}) copy-start(f32[8,256]{1,0:T(8,128)} %current_ref.3) | copy-start | bytes 24580
  52.7 19.4 %all-to-all-start.1 = ((f32[32,2,8,128]{3,2,1,0:T(8,128)}), f32[32,2,8,128]{3,2,1,0:T(8,128)S(1)}, u32[]{:S(2)}, u32[]{:S(2)}) async-start(f32[32,2,8,128]{3,2,1,0:T(8,128)} %copy-done.5), calls=%async_computation.1 | async-start | bytes 524288 | tf_op jit(solution)/shard_map/all_to_all | solution.py:20
  62.6 0.7 copy-start.8
  91.0 0.7 copy-start.11
  91.7 0.7 copy-start.14
  92.4 0.7 copy-start.25
  93.4 29.5 %copy-start.23 = (f32[8,256]{1,0:T(8,128)}, f32[8,256]{1,0:T(8,128)S(1)}, u32[]{:S(2)}) copy-start(f32[8,256]{1,0:T(8,128)S(1)} %get-tuple-element.14.applied_ref) | copy-start | bytes 24580
  108.7 14.2 %copy-start.3 = (bf16[32,16,128]{2,1,0:T(8,128)(2,1)}, bf16[32,16,128]{2,1,0:T(8,128)(2,1)S(1)}, u32[]{:S(2)}) copy-start(bf16[32,16,128]{2,1,0:T(8,128)(2,1)S(1)} %all_to_all.42.near_ref.vectors_ref) | copy-start | bytes 393220
  122.9 0.7 copy-start.12
  129.7 0.7 copy-start.2
  130.5 16.7 %all-to-all-start.6 = ((f32[32,3,8,128]{3,2,1,0:T(8,128)}), f32[32,3,8,128]{3,2,1,0:T(8,128)S(1)}, u32[]{:S(2)}, u32[]{:S(2)}) async-start(f32[32,3,8,128]{3,2,1,0:T(8,128)} %copy-done.2), calls=%async_computation.6 | async-start | bytes 786432 | tf_op jit(solution)/shard_map/all_to_all | solution.py:20
  134.3 0.9 copy-start.4
  138.8 0.7 copy-start.6
  147.2 1.0 copy-start.7
  171.1 0.7 copy-start.13
  171.8 0.7 copy-start.24
  (5 other events, 3.3 us)

commit v3 on v2

v3 whole, which is shorter than its diff:
```python
import functools

import jax
import jax.numpy as jnp
from jax import lax
from jax.experimental import pallas as pl
from jax.experimental.pallas import tpu as pltpu
from jax.sharding import PartitionSpec as P

HIGHEST = lax.Precision.HIGHEST
F32 = jnp.float32
BF16 = jnp.bfloat16
SHIFT = 1.25
VMEM = pl.BlockSpec(memory_space=pltpu.VMEM)
SMEM = pl.BlockSpec(memory_space=pltpu.SMEM)
PARAMS = pltpu.CompilerParams(vmem_limit_bytes=24 * 1024 * 1024)


def exchange(chunks, axis):
    return lax.all_to_all(chunks, axis, split_axis=0, concat_axis=0, tiled=True)


def call(kernel, out_shape, in_specs, scratch=()):
    many = isinstance(out_shape, (list, tuple))
    return pl.pallas_call(
        kernel,
        out_shape=out_shape,
        in_specs=in_specs,
        out_specs=tuple(VMEM for _ in out_shape) if many else VMEM,
        scratch_shapes=list(scratch),
        compiler_params=PARAMS,
    )


def shape_of(shape, dtype=F32):
    return jax.ShapeDtypeStruct(shape, dtype)


def pieces(ref):
    width = ref.shape[-1] // 2
    return [ref[:, :width], ref[:, width:]]


def contract_last(left, right):
    return lax.dot_general(
        left, right, (((1,), (1,)), ((), ())), precision=HIGHEST, preferred_element_type=F32
    )


def small_dot(left, right):
    total = left[:, 0:1] * right[0:1, :]
    for k in range(1, right.shape[0]):
        total = total + left[:, k : k + 1] * right[k : k + 1, :]
    return total


def identity(size):
    rows = lax.broadcasted_iota(jnp.int32, (size, size), 0)
    return (rows == lax.broadcasted_iota(jnp.int32, (size, size), 1)).astype(F32)


def split_three(values):
    high = values.astype(BF16)
    rest = values - high.astype(F32)
    middle = rest.astype(BF16)
    return high, middle, (rest - middle.astype(F32)).astype(BF16)


def pack_extra(values, shape):
    parts = [piece[:, :80].astype(F32) for piece in split_three(values)]
    top = jnp.concatenate([parts[0], parts[1][:, :48]], axis=1)
    zeros = jnp.zeros((shape[0] // 2, shape[1] - 32 - 80), F32)
    bottom = jnp.concatenate([parts[2], parts[1][:, 48:80], zeros], axis=1)
    return jnp.concatenate([top, bottom], axis=0).astype(BF16)


def unpack_extra(total):
    nv = total.shape[0] // 2
    top, bottom = total[:nv], total[nv:]
    middle = jnp.concatenate([top[:, 80:128], bottom[:, 80:112]], axis=1)
    return top[:, :80] + (middle + bottom[:, :80])


def rounded_kernel(vectors_ref, out_ref):
    chunk = jnp.concatenate(pieces(vectors_ref), axis=0).astype(BF16)
    out_ref[...] = jnp.broadcast_to(chunk[None], out_ref.shape)


def pack_kernel(current_ref, previous_ref, beta_ref, diagonal_ref, out_ref):
    nv = current_ref.shape[0]
    out_ref[:nv] = current_ref[...]
    out_ref[nv : 2 * nv] = small_dot(beta_ref[...], previous_ref[...])
    out_ref[2 * nv :] = jnp.broadcast_to(diagonal_ref[...], (nv, out_ref.shape[1]))


def multiply_slots(lists_ref, src, vectors_ref, blocks_ref, products_ref, over_columns):
    dims = (((1,), (1 if over_columns else 0,)), ((), ()))
    for k in range(blocks_ref.shape[0]):
        pair = vectors_ref[lax.shift_right_logical(lists_ref[src + k], 1)]
        products_ref[k] = lax.dot_general(
            pair, blocks_ref[k], dims, preferred_element_type=F32
        )


def products_into(over_columns, lists_ref, vectors_ref, blocks_ref, out_ref, products_ref):
    slots = blocks_ref.shape[0]
    src, dst = (slots, 0) if over_columns else (0, slots)
    nv = out_ref.shape[2]
    multiply_slots(lists_ref, src, vectors_ref, blocks_ref, products_ref, over_columns)
    out_ref[...] = jnp.zeros_like(out_ref)

    def one_slot(k, carry):
        half = pl.multiple_of((lists_ref[src + k] & 1) * nv, nv)
        block = lists_ref[dst + k]
        out_ref[lax.shift_right_logical(block, 1), block & 1] += products_ref[
            k, pl.ds(half, nv), :
        ]
        return carry

    lax.fori_loop(0, lists_ref[2 * slots], one_slot, 0)


def pair_of(ref, n):
    return jnp.concatenate([ref[n, 0], ref[n, 1]], axis=0)


def rounded_products_kernel(
    over_columns, lists_ref, vectors_ref, blocks_ref, out_ref, products_ref, sums_ref
):
    products_into(over_columns, lists_ref, vectors_ref, blocks_ref, sums_ref, products_ref)
    for n in range(out_ref.shape[0]):
        out_ref[n] = pair_of(sums_ref, n).astype(BF16)


def near_kernel(
    lists_ref, vectors_ref, near_ref, blocks_ref, state_ref, out_ref, products_ref, sums_ref
):
    products_into(True, lists_ref, vectors_ref, blocks_ref, sums_ref, products_ref)
    nv, width = sums_ref.shape[2:]
    total = jnp.zeros((4 * nv, 2 * nv), F32)
    for n in range(out_ref.shape[0]):
        pair = pair_of(sums_ref, n)
        high = pair.astype(BF16)
        low = (pair - high.astype(F32)).astype(BF16)
        out_ref[n, 0] = high
        total = total + lax.dot_general(
            jnp.concatenate([high, low], axis=0),
            near_ref[n],
            (((1,), (1,)), ((), ())),
            preferred_element_type=F32,
        )
    total = total[: 2 * nv] + total[2 * nv :]
    quadratic = total[:nv, :nv] + total[nv:, nv:]
    quadratic = quadratic + contract_last(identity(nv), quadratic)
    shifted = state_ref[nv : 2 * nv]
    quadratic = quadratic + contract_last(shifted, state_ref[3 * nv : 4 * nv] * shifted)
    used = 9 * nv
    extra = jnp.concatenate(
        [
            state_ref[4 * nv :, :used],
            quadratic,
            jnp.zeros((nv, width - used - nv), F32),
        ],
        axis=1,
    )
    packed = pack_extra(extra, (2 * nv, width))
    for n in range(out_ref.shape[0]):
        out_ref[n, 1] = packed


def middle_kernel(near_ref, far_ref, constants_ref, state_ref, payload_ref):
    nv, width = near_ref.shape[2:]
    total = jnp.zeros((3 * nv, 3 * nv), F32)
    halves = []
    for t in range(2):
        part = slice(t * width, (t + 1) * width)
        current = constants_ref[:nv, part]
        diag = constants_ref[2 * nv :, part]
        off_diagonal = jnp.sum(near_ref[:, t], axis=0) + jnp.sum(far_ref[:, t], axis=0)
        applied = off_diagonal + diag * current
        shifted = applied - constants_ref[nv : 2 * nv, part] - SHIFT * current
        stack = jnp.concatenate([current, shifted, applied], axis=0)
        state_ref[: 3 * nv, part] = stack
        state_ref[3 * nv : 4 * nv, part] = diag
        total = total + contract_last(stack, stack)
        halves.append(shifted)
    chunk = jnp.concatenate(halves, axis=0).astype(BF16)
    payload_ref[...] = jnp.broadcast_to(chunk[None], payload_ref.shape)
    state_ref[4 * nv :] = jnp.concatenate(
        [
            total[:nv],
            total[nv : 2 * nv],
            total[2 * nv :],
            jnp.zeros((nv, 2 * width - 9 * nv), F32),
        ],
        axis=1,
    )


def forward_kernel(near_ref, far_ref, sum_ref, out_ref):
    nv, width = sum_ref.shape[1:]
    total = jnp.sum(near_ref[:, 0].astype(F32), axis=0)
    sum_ref[0] = total[:nv]
    sum_ref[1] = total[nv:]
    extra = unpack_extra(jnp.sum(near_ref[:, 1].astype(F32), axis=0))
    extra = jnp.concatenate([extra, jnp.zeros((nv, width - 80), F32)], axis=1)
    out_ref[:, 0] = far_ref[...]
    out_ref[:, 1] = jnp.broadcast_to(
        pack_extra(extra, (2 * nv, width))[None], out_ref[:, 1].shape
    )


def last_kernel(
    rows_total, near_ref, far_ref, state_ref, residual_ref, next_ref, coefficients_ref
):
    nv, width = near_ref.shape[1:]
    far_sum = jnp.sum(far_ref[:, 0].astype(F32), axis=0)
    extra = unpack_extra(jnp.sum(far_ref[:, 1].astype(F32), axis=0))
    gram = lambda i: extra[:, i * nv : (i + 1) * nv]
    cc, cx, cu, xc, xx, xu, _, ux, _, xw = (gram(i) for i in range(10))
    eye = identity(nv)
    scale = 1.0 / rows_total
    alpha_one = (cx + SHIFT * cc) * scale
    alpha = alpha_one - SHIFT * eye
    alpha_t = (xc + SHIFT * cc) * scale - SHIFT * eye
    adjusted_c = xc - small_dot(alpha_t, cc)
    work = (xx - small_dot(alpha_t, cx) - small_dot(adjusted_c, alpha)) * scale
    rows = lax.broadcasted_iota(jnp.int32, (nv, nv), 0)
    columns = lax.broadcasted_iota(jnp.int32, (nv, nv), 1)
    factor = jnp.zeros((nv, nv), F32)
    factor_t = jnp.zeros((nv, nv), F32)
    inverse = eye
    for j in range(nv):
        root = lax.rsqrt(work[j : j + 1, j : j + 1])
        column = jnp.where(rows[:, :1] >= j, work[:, j : j + 1] * root, 0.0)
        row = jnp.where(columns[:1] >= j, work[j : j + 1, :] * root, 0.0)
        factor = jnp.where(columns == j, column, factor)
        factor_t = jnp.where(rows == j, row, factor_t)
        work = work - column * row
        done = inverse[j : j + 1, :] * root
        below = jnp.where(rows[:, :1] > j, column, 0.0)
        inverse = jnp.where(rows == j, done, inverse - below * done)
    z = (
        xw
        - small_dot(xu, alpha)
        - small_dot(alpha_t, ux)
        + small_dot(small_dot(alpha_t, cu), alpha)
    )
    alpha_two = contract_last(small_dot(inverse, z), inverse)
    alpha_two = (alpha_two - small_dot(small_dot(inverse, adjusted_c), factor)) * scale
    alpha_two_t = contract_last(eye, alpha_two)
    for t in range(2):
        part = slice(t * width, (t + 1) * width)
        current = state_ref[:nv, part]
        shifted = state_ref[nv : 2 * nv, part]
        applied = state_ref[2 * nv : 3 * nv, part]
        applied_shifted = near_ref[t] + far_sum[t * nv : (t + 1) * nv]
        applied_shifted = applied_shifted + state_ref[3 * nv : 4 * nv, part] * shifted
        following = small_dot(inverse, shifted - small_dot(alpha_t, current))
        second = small_dot(inverse, applied_shifted - small_dot(alpha_t, applied))
        second = second - small_dot(factor_t, current)
        next_ref[:, part] = following
        residual_ref[:, part] = second - small_dot(alpha_two_t, following)
    coefficients_ref[0] = alpha_one
    coefficients_ref[1] = factor
    coefficients_ref[2] = alpha_two


def on_device(
    current_block, previous_block, beta_coupling, diagonal, blocks, near_index, far_index, counts
):
    tile_blocks = blocks[0, 0]
    lists = jnp.concatenate([near_index[0, 0], far_index[0, 0], counts[0]])
    nv, share = current_block.shape
    slots, width = tile_blocks.shape[:2]
    n_row, n_col = lax.axis_size("row"), lax.axis_size("col")
    rows_total = share * n_row * n_col
    products_scratch = pltpu.VMEM((slots, 2 * nv, width), F32)

    chunks = call(rounded_kernel, shape_of((n_col, 2 * nv, width), BF16), [VMEM])(current_block)
    constants = call(pack_kernel, shape_of((3 * nv, share)), [VMEM] * 4)(
        current_block, previous_block, beta_coupling, diagonal.reshape(1, share)
    )
    near_vectors = exchange(chunks, "col")
    far_vectors = exchange(chunks, "row")

    def products(over_columns, vectors, peers):
        return call(
            functools.partial(products_into, over_columns),
            shape_of((peers, 2, nv, width)),
            [SMEM, VMEM, VMEM],
            [products_scratch],
        )(lists, vectors, tile_blocks)

    far_got = exchange(products(False, near_vectors, n_row), "row")
    near_got = exchange(products(True, far_vectors, n_col), "col")
    state, chunks = call(
        middle_kernel,
        (shape_of((5 * nv, share)), shape_of((n_col, 2 * nv, width), BF16)),
        [VMEM] * 3,
    )(near_got, far_got, constants)

    near_vectors = exchange(chunks, "col")
    chunks, near_vectors = lax.optimization_barrier((chunks, near_vectors))
    far_vectors = exchange(chunks, "row")
    far_part = call(
        functools.partial(rounded_products_kernel, False),
        shape_of((n_row, 2 * nv, width), BF16),
        [SMEM, VMEM, VMEM],
        [products_scratch, pltpu.VMEM((n_row, 2, nv, width), F32)],
    )(lists, near_vectors, tile_blocks)
    near_part = call(
        near_kernel,
        shape_of((n_col, 2, 2 * nv, width), BF16),
        [SMEM] + [VMEM] * 4,
        [products_scratch, pltpu.VMEM((n_col, 2, nv, width), F32)],
    )(lists, far_vectors, near_vectors, tile_blocks, state)
    near_got = exchange(near_part, "col")
    near_sum, far_part = call(
        forward_kernel,
        (shape_of((2, nv, width)), shape_of((n_row, 2, 2 * nv, width), BF16)),
        [VMEM] * 2,
    )(near_got, far_part)
    far_got = exchange(far_part, "row")
    return call(
        functools.partial(last_kernel, rows_total),
        (shape_of((nv, share)), shape_of((nv, share)), shape_of((3, nv, nv))),
        [VMEM] * 3,
    )(near_sum, far_got, state)


def solution(mesh):
    return jax.shard_map(
        on_device,
        mesh=mesh,
        in_specs=(
            P(None, ("row", "col")),
            P(None, ("row", "col")),
            P(),
            P(("row", "col")),
            P("row", "col", None, None, None),
            P("row", "col", None),
            P("row", "col", None),
            P("row", "col"),
        ),
        out_specs=(P(None, ("row", "col")), P(None, ("row", "col")), P()),
        check_vma=False,
    )
```

time: 177 us -> 166 us (0.938)
  blocking collectives: 99.1 us -> 75.6 us
  waiting for transfers between devices: 20.1 us -> 31.9 us
  starting transfers between devices: 23.2 us -> 31.4 us
  local copies, waits for them, and re-layouts: 15.3 us -> 7.67 us
    all_to_all x5 -> x4, blocking collectives: 99.1 us -> 75.6 us  [exchange(): return lax.all_to_all(chunks, axis, split_axis=0, concat_axis=0, tiled=True)]
    all_to_all x3 -> x4, waiting for transfers between devices: 20.1 us -> 31.9 us  [exchange(): return lax.all_to_all(chunks, axis, split_axis=0, concat_axis=0, tiled=True)]
    all_to_all x3 -> x4, starting transfers between devices: 23.2 us -> 31.4 us  [exchange(): return lax.all_to_all(chunks, axis, split_axis=0, concat_axis=0, tiled=True)]
    unnamed x52 -> x26, local copies, waits for them, and re-layouts: 15.3 us -> 7.67 us
    pallas_call x7 -> x8, Pallas kernels: 15.9 us -> 16.2 us  [the longest x2 5.04 us: products(): call(functools.partial(products_into, over_columns), shape_of((peers, 2,...]
  transfers between devices with their start and end apart: 3 -> 4, of which waited for: 3 -> 4; matrix products, arithmetic and copies ran while one was open for 0% -> 0% of each run, Pallas kernels for 4% -> 4%
where the time goes in v3:
time: 166 us
  blocking collectives  75.6 us (46%)
  waiting for transfers between devices  31.9 us (19%)
  starting transfers between devices  31.4 us (19%)
  Pallas kernels  16.9 us (10%)
  local copies, waits for them, and re-layouts  7.67 us (5%)
    all_to_all x4, blocking collectives, exchange(): return lax.all_to_all(chunks, axis, split_axis=0, concat_axis=0, tiled=True)  75.6 us
    all_to_all x4, waiting for transfers between devices, exchange(): return lax.all_to_all(chunks, axis, split_axis=0, concat_axis=0, tiled=True)  31.9 us
    all_to_all x4, starting transfers between devices, exchange(): return lax.all_to_all(chunks, axis, split_axis=0, concat_axis=0, tiled=True)  31.4 us
    unnamed x26, local copies, waits for them, and re-layouts  7.67 us
    pallas_call x2, Pallas kernels, products(): call(functools.partial(products_into, over_columns), shape_of((peers, 2,...  5.04 us
    pallas_call x1, Pallas kernels, on_device(): call(near_kernel, shape_of((n_col, 2, 2 * nv, width), BF16), [SMEM] + [VM...  4.38 us
  transfers between devices with their start and end apart: 4, of which 4 were waited for; matrix products, arithmetic and copies ran while one was open for 0% of the time, Pallas kernels for 4%

profile of v3, /device:TPU:1, one launch (start us, length us, event | category | flops | bytes accessed | tf_op | source)
XLA Modules:
  0.0 165.6 jit_solution(5415882302747252228)
XLA Ops:
  2.0 27.7 %all_to_all.40.vectors_ref = bf16[32,16,128]{2,1,0:T(8,128)(2,1)S(1)} all-to-all(bf16[32,16,128]{2,1,0:T(8,128)(2,1)} %shard_map.103), channel_id=1, replica_groups=mesh['row'=32,'col'=32] {'row'}, dimensions={0} | all-to-all | bytes 262144 | tf_op jit(solution)/shard_map/all_to_all | solution.py:20
  29.7 11.7 %all-to-all-start.2 = ((bf16[32,16,128]{2,1,0:T(8,128)(2,1)}), bf16[32,16,128]{2,1,0:T(8,128)(2,1)S(1)}, u32[]{:S(2)}, u32[]{:S(2)}) async-start(bf16[32,16,128]{2,1,0:T(8,128)(2,1)} %shard_map.103), calls=%async_computation.2 | async-start | bytes 262144 | tf_op jit(solution)/shard_map/all_to_all | solution.py:20
  42.1 0.7 pad_add_fusion.lists_ref
  42.8 1.9 %copy-done = bf16[1,1,96,128,128]{4,3,2,1,0:T(8,128)(2,1)S(1)} copy-done((bf16[1,1,96,128,128]{4,3,2,1,0:T(8,128)(2,1)S(1)}, bf16[1,1,96,128,128]{4,3,2,1,0:T(8,128)(2,1)}, u32[]{:S(2)}) %copy-start) | copy-done | bytes 3145752
  44.7 2.9 %shard_map.104 = f32[32,2,8,128]{3,2,1,0:T(8,128)S(1)} custom-call(s32[193]{0:T(256)S(1)} %pad_add_fusion.lists_ref, bf16[32,16,128]{2,1,0:T(8,128)(2,1)S(1)} %all_to_all.40.vectors_ref, bf16[96,128,128]{2,1,0:T(8,128)(2,1)S(1)} %bitcast.6), custom_call_target="tpu_custom_call" | custom-call | tf_op jit(solution)/shard_map/pallas_call | solution.py:288
  47.7 0.7 copy-done.2
  48.3 4.3 %all-to-all-done.2.vectors_ref = bf16[32,16,128]{2,1,0:T(8,128)(2,1)S(1)} async-done(((bf16[32,16,128]{2,1,0:T(8,128)(2,1)}), bf16[32,16,128]{2,1,0:T(8,128)(2,1)S(1)}, u32[]{:S(2)}, u32[]{:S(2)}) %all-to-all-start.2) | async-done | bytes 131104 | tf_op jit(solution)/shard_map/all_to_all | solution.py:20
  52.7 7.5 %all-to-all-start.1 = ((f32[32,2,8,128]{3,2,1,0:T(8,128)}), f32[32,2,8,128]{3,2,1,0:T(8,128)S(1)}, u32[]{:S(2)}, u32[]{:S(2)}) async-start(f32[32,2,8,128]{3,2,1,0:T(8,128)} %copy-done.2), calls=%async_computation.1 | async-start | bytes 524288 | tf_op jit(solution)/shard_map/all_to_all | solution.py:20
  60.2 2.1 %shard_map.105 = f32[32,2,8,128]{3,2,1,0:T(8,128)S(1)} custom-call(s32[193]{0:T(256)S(1)} %pad_add_fusion.lists_ref, bf16[32,16,128]{2,1,0:T(8,128)(2,1)S(1)} %all-to-all-done.2.vectors_ref, bf16[96,128,128]{2,1,0:T(8,128)(2,1)S(1)} %bitcast.7), custom_call_target="tpu_custom_call" | custom-call | tf_op jit(solution)/shard_map/pallas_call | solution.py:288
  62.3 0.7 copy-done.3
  63.0 9.0 %all-to-all-done.1.near_ref = f32[32,2,8,128]{3,2,1,0:T(8,128)S(1)} async-done(((f32[32,2,8,128]{3,2,1,0:T(8,128)}), f32[32,2,8,128]{3,2,1,0:T(8,128)S(1)}, u32[]{:S(2)}, u32[]{:S(2)}) %all-to-all-start.1) | async-done | bytes 262176 | tf_op jit(solution)/shard_map/all_to_all | solution.py:20
  72.0 8.3 %all-to-all-start.3 = ((f32[32,2,8,128]{3,2,1,0:T(8,128)}), f32[32,2,8,128]{3,2,1,0:T(8,128)}, u32[]{:S(2)}, u32[]{:S(2)}) async-start(f32[32,2,8,128]{3,2,1,0:T(8,128)} %copy-done.3), calls=%async_computation.3 | async-start | bytes 524288 | tf_op jit(solution)/shard_map/all_to_all | solution.py:20
  81.8 9.6 %all-to-all-done.3.far_ref = f32[32,2,8,128]{3,2,1,0:T(8,128)} async-done(((f32[32,2,8,128]{3,2,1,0:T(8,128)}), f32[32,2,8,128]{3,2,1,0:T(8,128)}, u32[]{:S(2)}, u32[]{:S(2)}) %all-to-all-start.3) | async-done | bytes 262176 | tf_op jit(solution)/shard_map/all_to_all | solution.py:20
  91.4 1.2 shard_map.107
  92.7 15.1 %all_to_all.41.near_ref.vectors_ref = bf16[32,16,128]{2,1,0:T(8,128)(2,1)S(1)} all-to-all(bf16[32,16,128]{2,1,0:T(8,128)(2,1)S(1)} %get-tuple-element.10), channel_id=1, replica_groups=mesh['row'=32,'col'=32] {'col'}, dimensions={0} | all-to-all | bytes 262144 | tf_op jit(solution)/shard_map/all_to_all | solution.py:20
  107.8 14.3 %all_to_all.42.vectors_ref = bf16[32,16,128]{2,1,0:T(8,128)(2,1)S(1)} all-to-all(bf16[32,16,128]{2,1,0:T(8,128)(2,1)S(1)} %get-tuple-element.10), channel_id=1, replica_groups=mesh['row'=32,'col'=32] {'row'}, dimensions={0} | all-to-all | bytes 262144 | tf_op jit(solution)/shard_map/all_to_all | solution.py:20
  122.1 4.4 %shard_map.108 = bf16[32,2,16,128]{3,2,1,0:T(8,128)(2,1)} custom-call(s32[193]{0:T(256)S(1)} %pad_add_fusion.lists_ref, bf16[32,16,128]{2,1,0:T(8,128)(2,1)S(1)} %all_to_all.42.vectors_ref, bf16[32,16,128]{2,1,0:T(8,128)(2,1)S(1)} %all_to_all.41.near_ref.vectors_ref, bf16[96,128,128]{2,1,0:T(8,128)(2,1)S(1)} %bitcast.8, ...), custom_call_target="tpu_custom_call" | custom-call | tf_op jit(solution)/shard_map/pallas_call | solution.py:312
  126.5 3.9 %all-to-all-start.6 = ((bf16[32,2,16,128]{3,2,1,0:T(8,128)(2,1)}), bf16[32,2,16,128]{3,2,1,0:T(8,128)(2,1)S(1)}, u32[]{:S(2)}, u32[]{:S(2)}) async-start(bf16[32,2,16,128]{3,2,1,0:T(8,128)(2,1)} %shard_map.108), calls=%async_computation.6 | async-start | bytes 524288 | tf_op jit(solution)/shard_map/all_to_all | solution.py:20
  130.3 2.1 %shard_map.109.far_ref = bf16[32,16,128]{2,1,0:T(8,128)(2,1)S(1)} custom-call(s32[193]{0:T(256)S(1)} %pad_add_fusion.lists_ref, bf16[32,16,128]{2,1,0:T(8,128)(2,1)S(1)} %all_to_all.41.near_ref.vectors_ref, bf16[96,128,128]{2,1,0:T(8,128)(2,1)S(1)} %bitcast.9), custom_call_target="tpu_custom_call" | custom-call | tf_op jit(solution)/shard_map/pallas_call | solution.py:306
  133.1 9.0 %all-to-all-done.6.near_ref = bf16[32,2,16,128]{3,2,1,0:T(8,128)(2,1)S(1)} async-done(((bf16[32,2,16,128]{3,2,1,0:T(8,128)(2,1)}), bf16[32,2,16,128]{3,2,1,0:T(8,128)(2,1)S(1)}, u32[]{:S(2)}, u32[]{:S(2)}) %all-to-all-start.6) | async-done | bytes 262176 | tf_op jit(solution)/shard_map/all_to_all | solution.py:20
  142.1 0.9 copy-done.5
  143.2 18.4 %all_to_all.43.far_ref = bf16[32,2,16,128]{3,2,1,0:T(8,128)(2,1)S(1)} all-to-all(bf16[32,2,16,128]{3,2,1,0:T(8,128)(2,1)S(1)} %get-tuple-element.14), channel_id=1, replica_groups=mesh['row'=32,'col'=32] {'row'}, dimensions={0} | all-to-all | bytes 524288 | tf_op jit(solution)/shard_map/all_to_all | solution.py:20
  161.6 0.8 copy-done.7
  162.4 3.2 %shard_map.111 = (f32[8,256]{1,0:T(8,128)}, f32[8,256]{1,0:T(8,128)}, f32[3,8,8]{2,1,0:T(8,128)}) custom-call(f32[2,8,128]{2,1,0:T(8,128)S(1)} %get-tuple-element.13.near_ref, bf16[32,2,16,128]{3,2,1,0:T(8,128)(2,1)S(1)} %all_to_all.43.far_ref, f32[40,256]{1,0:T(8,128)S(1)} %copy-done.7), custom_call_target="tpu_custom_call" | custom-call | tf_op jit(solution)/shard_map/pallas_call | solution.py:325
  (24 shorter events, 3.6 us)
Async XLA Ops:
  0.6 0.7 copy-start.8
  29.7 22.9 %all-to-all-start.2 = ((bf16[32,16,128]{2,1,0:T(8,128)(2,1)}), bf16[32,16,128]{2,1,0:T(8,128)(2,1)S(1)}, u32[]{:S(2)}, u32[]{:S(2)}) async-start(bf16[32,16,128]{2,1,0:T(8,128)(2,1)} %shard_map.103), calls=%async_computation.2 | async-start | bytes 262144 | tf_op jit(solution)/shard_map/all_to_all | solution.py:20
  42.8 1.9 %copy-start = (bf16[1,1,96,128,128]{4,3,2,1,0:T(8,128)(2,1)S(1)}, bf16[1,1,96,128,128]{4,3,2,1,0:T(8,128)(2,1)}, u32[]{:S(2)}) copy-start(bf16[1,1,96,128,128]{4,3,2,1,0:T(8,128)(2,1)} %param.12) | copy-start | bytes 9437188
  44.7 15.5 %copy-start.1 = (bf16[1,1,96,128,128]{4,3,2,1,0:T(8,128)(2,1)S(1)}, bf16[1,1,96,128,128]{4,3,2,1,0:T(8,128)(2,1)}, u32[]{:S(2)}) copy-start(bf16[1,1,96,128,128]{4,3,2,1,0:T(8,128)(2,1)} %param.12) | copy-start | bytes 9437188
  47.6 0.7 copy-start.2
  48.3 32.0 %copy-start.9 = (f32[8,256]{1,0:T(8,128)S(1)}, f32[8,256]{1,0:T(8,128)}, u32[]{:S(2)}) copy-start(f32[8,256]{1,0:T(8,128)} %current_ref.1) | copy-start | bytes 24580
  48.3 32.0 %copy-start.11 = (f32[8,8]{1,0:T(8,128)S(1)}, f32[8,8]{1,0:T(8,128)}, u32[]{:S(2)}) copy-start(f32[8,8]{1,0:T(8,128)} %beta_ref.1) | copy-start | bytes 772
  52.7 19.3 %all-to-all-start.1 = ((f32[32,2,8,128]{3,2,1,0:T(8,128)}), f32[32,2,8,128]{3,2,1,0:T(8,128)S(1)}, u32[]{:S(2)}, u32[]{:S(2)}) async-start(f32[32,2,8,128]{3,2,1,0:T(8,128)} %copy-done.2), calls=%async_computation.1 | async-start | bytes 524288 | tf_op jit(solution)/shard_map/all_to_all | solution.py:20
  62.3 0.7 copy-start.3
  72.0 19.4 %all-to-all-start.3 = ((f32[32,2,8,128]{3,2,1,0:T(8,128)}), f32[32,2,8,128]{3,2,1,0:T(8,128)}, u32[]{:S(2)}, u32[]{:S(2)}) async-start(f32[32,2,8,128]{3,2,1,0:T(8,128)} %copy-done.3), calls=%async_computation.3 | async-start | bytes 524288 | tf_op jit(solution)/shard_map/all_to_all | solution.py:20
  80.3 0.7 copy-start.10
  81.0 0.7 copy-start.12
  92.7 29.4 %copy-start.6 = (f32[40,256]{1,0:T(8,128)}, f32[40,256]{1,0:T(8,128)S(1)}, u32[]{:S(2)}) copy-start(f32[40,256]{1,0:T(8,128)S(1)} %get-tuple-element.12.state_ref) | copy-start | bytes 122884
  126.5 15.6 %all-to-all-start.6 = ((bf16[32,2,16,128]{3,2,1,0:T(8,128)(2,1)}), bf16[32,2,16,128]{3,2,1,0:T(8,128)(2,1)S(1)}, u32[]{:S(2)}, u32[]{:S(2)}) async-start(bf16[32,2,16,128]{3,2,1,0:T(8,128)(2,1)} %shard_map.108), calls=%async_computation.6 | async-start | bytes 524288 | tf_op jit(solution)/shard_map/all_to_all | solution.py:20
  132.5 0.6 copy-start.4
  142.1 0.9 copy-start.5
  161.6 0.8 copy-start.7

commit v4 on v3

v4 whole, which is shorter than its diff:
```python
import functools

import jax
import jax.numpy as jnp
from jax import lax
from jax.experimental import pallas as pl
from jax.experimental.pallas import tpu as pltpu
from jax.sharding import PartitionSpec as P

HIGHEST = lax.Precision.HIGHEST
F32 = jnp.float32
BF16 = jnp.bfloat16
SHIFT = 1.25
VMEM = pl.BlockSpec(memory_space=pltpu.VMEM)
SMEM = pl.BlockSpec(memory_space=pltpu.SMEM)
PARAMS = pltpu.CompilerParams(vmem_limit_bytes=24 * 1024 * 1024)


def exchange(chunks, axis):
    return lax.all_to_all(chunks, axis, split_axis=0, concat_axis=0, tiled=True)


def call(kernel, out_shape, in_specs, scratch=()):
    many = isinstance(out_shape, (list, tuple))
    return pl.pallas_call(
        kernel,
        out_shape=out_shape,
        in_specs=in_specs,
        out_specs=tuple(VMEM for _ in out_shape) if many else VMEM,
        scratch_shapes=list(scratch),
        compiler_params=PARAMS,
    )


def shape_of(shape, dtype=F32):
    return jax.ShapeDtypeStruct(shape, dtype)


def pieces(ref):
    width = ref.shape[-1] // 2
    return [ref[:, :width], ref[:, width:]]


def contract_last(left, right):
    return lax.dot_general(
        left, right, (((1,), (1,)), ((), ())), precision=HIGHEST, preferred_element_type=F32
    )


def small_dot(left, right):
    total = left[:, 0:1] * right[0:1, :]
    for k in range(1, right.shape[0]):
        total = total + left[:, k : k + 1] * right[k : k + 1, :]
    return total


def identity(size):
    rows = lax.broadcasted_iota(jnp.int32, (size, size), 0)
    return (rows == lax.broadcasted_iota(jnp.int32, (size, size), 1)).astype(F32)


def split_two(values):
    high = values.astype(BF16)
    return high, (values - high.astype(F32)).astype(BF16)


def pack_extra(extra):
    high = extra.astype(BF16).astype(F32)
    rest = extra - high
    middle = rest.astype(BF16).astype(F32)
    low = rest - middle
    nv = extra.shape[0]
    return jnp.concatenate([high, middle, low[:, : 4 * nv]], axis=1)


def unpack_extra(total):
    nv = total.shape[0]
    low = jnp.concatenate([total[:, 12 * nv :], jnp.zeros((nv, 2 * nv), F32)], axis=1)
    return total[:, : 6 * nv] + (total[:, 6 * nv : 12 * nv] + low)


def rounded_kernel(vectors_ref, out_ref):
    chunk = jnp.concatenate(pieces(vectors_ref), axis=0).astype(BF16)
    out_ref[...] = jnp.broadcast_to(chunk[None], out_ref.shape)


def pack_kernel(current_ref, previous_ref, beta_ref, diagonal_ref, out_ref):
    nv = current_ref.shape[0]
    out_ref[:nv] = current_ref[...]
    out_ref[nv : 2 * nv] = small_dot(beta_ref[...], previous_ref[...])
    out_ref[2 * nv :] = jnp.broadcast_to(diagonal_ref[...], (nv, out_ref.shape[1]))


def products_kernel(over_columns, lists_ref, vectors_ref, blocks_ref, out_ref, products_ref):
    slots = blocks_ref.shape[0]
    src, dst = (slots, 0) if over_columns else (0, slots)
    nv = out_ref.shape[2]
    has_low = vectors_ref.shape[1] > 2 * nv
    dims = (((1,), (1 if over_columns else 0,)), ((), ()))
    for k in range(slots):
        pair = vectors_ref[lax.shift_right_logical(lists_ref[src + k], 1)]
        product = lax.dot_general(pair, blocks_ref[k], dims, preferred_element_type=F32)
        if has_low:
            product = product[: 2 * nv] + product[2 * nv :]
        products_ref[k] = product
    out_ref[...] = jnp.zeros_like(out_ref)

    def one_slot(k, carry):
        half = pl.multiple_of((lists_ref[src + k] & 1) * nv, nv)
        block = lists_ref[dst + k]
        out_ref[lax.shift_right_logical(block, 1), block & 1] += products_ref[
            k, pl.ds(half, nv), :
        ]
        return carry

    lax.fori_loop(0, lists_ref[2 * slots], one_slot, 0)


def quadratic_kernel(sums_ref, near_ref, state_ref, out_ref):
    nv, width = sums_ref.shape[2:]
    total = jnp.zeros((4 * nv, 4 * nv), F32)
    for n in range(out_ref.shape[0]):
        pair = jnp.concatenate([sums_ref[n, 0], sums_ref[n, 1]], axis=0)
        high, low = split_two(pair)
        total = total + lax.dot_general(
            jnp.concatenate([high, low], axis=0),
            near_ref[n],
            (((1,), (1,)), ((), ())),
            preferred_element_type=F32,
        )
    total = total[: 2 * nv] + total[2 * nv :]
    total = total[:, : 2 * nv] + total[:, 2 * nv :]
    quadratic = total[:nv, :nv] + total[nv:, nv:]
    quadratic = quadratic + contract_last(identity(nv), quadratic)
    shifted = state_ref[nv : 2 * nv]
    quadratic = quadratic + contract_last(shifted, state_ref[3 * nv : 4 * nv] * shifted)
    extra = pack_extra(jnp.concatenate([state_ref[4 * nv :, : 5 * nv], quadratic], axis=1))
    for n in range(out_ref.shape[0]):
        out_ref[n] = jnp.concatenate([sums_ref[n, 0], sums_ref[n, 1], extra], axis=0).astype(BF16)


def middle_kernel(near_ref, far_ref, constants_ref, state_ref, payload_ref):
    nv, width = near_ref.shape[2:]
    total = jnp.zeros((3 * nv, 3 * nv), F32)
    halves = []
    for t in range(2):
        part = slice(t * width, (t + 1) * width)
        current = constants_ref[:nv, part]
        diag = constants_ref[2 * nv :, part]
        off_diagonal = jnp.sum(near_ref[:, t], axis=0) + jnp.sum(far_ref[:, t], axis=0)
        applied = off_diagonal + diag * current
        shifted = applied - constants_ref[nv : 2 * nv, part] - SHIFT * current
        stack = jnp.concatenate([current, shifted, applied], axis=0)
        state_ref[: 3 * nv, part] = stack
        state_ref[3 * nv : 4 * nv, part] = diag
        total = total + contract_last(stack, stack)
        halves.append(shifted)
    pair = jnp.concatenate(halves, axis=0)
    high = pair.astype(BF16).astype(F32)
    chunk = jnp.concatenate([high, pair - high], axis=0).astype(BF16)
    payload_ref[...] = jnp.broadcast_to(chunk[None], payload_ref.shape)
    state_ref[4 * nv :] = jnp.concatenate(
        [
            total[:nv, :nv],
            total[nv : 2 * nv, nv : 2 * nv],
            total[:nv, nv : 2 * nv],
            total[nv : 2 * nv, 2 * nv :],
            total[:nv, 2 * nv :],
            jnp.zeros((nv, 2 * width - 5 * nv), F32),
        ],
        axis=1,
    )


def forward_kernel(near_ref, far_ref, state_ref, late_ref, out_ref):
    nv = far_ref.shape[2]
    width = far_ref.shape[3]
    total = jnp.sum(near_ref[...].astype(F32), axis=0)
    late_ref[: 3 * nv] = state_ref[: 3 * nv]
    for t in range(2):
        part = slice(t * width, (t + 1) * width)
        late_ref[3 * nv :, part] = (
            total[t * nv : (t + 1) * nv] + state_ref[3 * nv : 4 * nv, part] * state_ref[nv : 2 * nv, part]
        )
    extra = pack_extra(unpack_extra(total[2 * nv :]))
    for n in range(out_ref.shape[0]):
        out_ref[n] = jnp.concatenate([far_ref[n, 0], far_ref[n, 1], extra], axis=0).astype(BF16)


def last_kernel(rows_total, far_ref, state_ref, residual_ref, next_ref, coefficients_ref):
    nv, width = coefficients_ref.shape[1], far_ref.shape[2]
    received = jnp.sum(far_ref[...].astype(F32), axis=0)
    extra = unpack_extra(received[2 * nv :])
    gram = lambda i: extra[:, i * nv : (i + 1) * nv]
    cc, xx, cx, xu, cu, xw = (gram(i) for i in range(6))
    eye = identity(nv)
    xc = contract_last(eye, cx)
    scale = 1.0 / rows_total
    alpha_one = (cx + SHIFT * cc) * scale
    alpha = alpha_one - SHIFT * eye
    alpha_t = (xc + SHIFT * cc) * scale - SHIFT * eye
    adjusted_c = xc - small_dot(alpha_t, cc)
    work = (xx - small_dot(alpha_t, cx) - small_dot(adjusted_c, alpha)) * scale
    rows = lax.broadcasted_iota(jnp.int32, (nv, nv), 0)
    columns = lax.broadcasted_iota(jnp.int32, (nv, nv), 1)
    factor = jnp.zeros((nv, nv), F32)
    factor_t = jnp.zeros((nv, nv), F32)
    inverse = eye
    for j in range(nv):
        root = lax.rsqrt(work[j : j + 1, j : j + 1])
        column = jnp.where(rows[:, :1] >= j, work[:, j : j + 1] * root, 0.0)
        row = jnp.where(columns[:1] >= j, work[j : j + 1, :] * root, 0.0)
        factor = jnp.where(columns == j, column, factor)
        factor_t = jnp.where(rows == j, row, factor_t)
        work = work - column * row
        done = inverse[j : j + 1, :] * root
        below = jnp.where(rows[:, :1] > j, column, 0.0)
        inverse = jnp.where(rows == j, done, inverse - below * done)
    half = small_dot(xu, alpha)
    z = (
        xw
        - half
        - contract_last(eye, half)
        + small_dot(small_dot(alpha_t, cu), alpha)
    )
    alpha_two = contract_last(small_dot(inverse, z), inverse)
    alpha_two = (alpha_two - small_dot(small_dot(inverse, adjusted_c), factor)) * scale
    alpha_two_t = contract_last(eye, alpha_two)
    for t in range(2):
        part = slice(t * width, (t + 1) * width)
        current = state_ref[:nv, part]
        shifted = state_ref[nv : 2 * nv, part]
        applied = state_ref[2 * nv : 3 * nv, part]
        applied_shifted = state_ref[3 * nv :, part] + received[t * nv : (t + 1) * nv]
        following = small_dot(inverse, shifted - small_dot(alpha_t, current))
        second = small_dot(inverse, applied_shifted - small_dot(alpha_t, applied))
        second = second - small_dot(factor_t, current)
        next_ref[:, part] = following
        residual_ref[:, part] = second - small_dot(alpha_two_t, following)
    coefficients_ref[0] = alpha_one
    coefficients_ref[1] = factor
    coefficients_ref[2] = alpha_two


def on_device(
    current_block, previous_block, beta_coupling, diagonal, blocks, near_index, far_index, counts
):
    tile_blocks = blocks[0, 0]
    lists = jnp.concatenate([near_index[0, 0], far_index[0, 0], counts[0]])
    nv, share = current_block.shape
    slots, width = tile_blocks.shape[:2]
    n_row, n_col = lax.axis_size("row"), lax.axis_size("col")
    rows_total = share * n_row * n_col

    def products(over_columns, vectors, peers):
        return call(
            functools.partial(products_kernel, over_columns),
            shape_of((peers, 2, nv, width)),
            [SMEM, VMEM, VMEM],
            [pltpu.VMEM((slots, 2 * nv, width), F32)],
        )(lists, vectors, tile_blocks)

    chunks = call(rounded_kernel, shape_of((n_col, 2 * nv, width), BF16), [VMEM])(current_block)
    constants = call(pack_kernel, shape_of((3 * nv, share)), [VMEM] * 4)(
        current_block, previous_block, beta_coupling, diagonal.reshape(1, share)
    )
    lists, constants = lax.optimization_barrier((lists, constants))
    near_vectors = exchange(chunks, "col")
    far_vectors = exchange(chunks, "row")
    far_got = exchange(products(False, near_vectors, n_row), "row")
    near_got = exchange(products(True, far_vectors, n_col), "col")
    state, chunks = call(
        middle_kernel,
        (shape_of((5 * nv, share)), shape_of((n_col, 4 * nv, width), BF16)),
        [VMEM] * 3,
    )(near_got, far_got, constants)

    far_vectors = exchange(chunks, "row")
    chunks, far_vectors = lax.optimization_barrier((chunks, far_vectors))
    near_vectors = exchange(chunks, "col")
    near_part = products(True, far_vectors, n_col)
    near_part = call(quadratic_kernel, shape_of((n_col, 3 * nv, width), BF16), [VMEM] * 3)(
        near_part, near_vectors, state
    )
    near_got = exchange(near_part, "col")
    far_part = products(False, near_vectors, n_row)
    late, far_part = call(
        forward_kernel,
        (shape_of((4 * nv, share)), shape_of((n_row, 3 * nv, width), BF16)),
        [VMEM] * 3,
    )(near_got, far_part, state)
    far_got = exchange(far_part, "row")
    return call(
        functools.partial(last_kernel, rows_total),
        (shape_of((nv, share)), shape_of((nv, share)), shape_of((3, nv, nv))),
        [VMEM] * 2,
    )(far_got, late)


def solution(mesh):
    return jax.shard_map(
        on_device,
        mesh=mesh,
        in_specs=(
            P(None, ("row", "col")),
            P(None, ("row", "col")),
            P(),
            P(("row", "col")),
            P("row", "col", None, None, None),
            P("row", "col", None),
            P("row", "col", None),
            P("row", "col"),
        ),
        out_specs=(P(None, ("row", "col")), P(None, ("row", "col")), P()),
        check_vma=False,
    )
```

time: 166 us -> 171 us (1.030)
  waiting for transfers between devices: 31.9 us -> 25.6 us
  local copies, waits for them, and re-layouts: 7.67 us -> 13.7 us
  blocking collectives: 75.6 us -> 79 us
  starting transfers between devices: 31.4 us -> 33.4 us
    all_to_all x4, waiting for transfers between devices: 31.9 us -> 25.6 us  [exchange(): return lax.all_to_all(chunks, axis, split_axis=0, concat_axis=0, tiled=True)]
    unnamed x26 -> x36, local copies, waits for them, and re-layouts: 7.67 us -> 13.7 us
    all_to_all x4, blocking collectives: 75.6 us -> 79 us  [exchange(): return lax.all_to_all(chunks, axis, split_axis=0, concat_axis=0, tiled=True)]
    all_to_all x4, starting transfers between devices: 31.4 us -> 33.4 us  [exchange(): return lax.all_to_all(chunks, axis, split_axis=0, concat_axis=0, tiled=True)]
    pallas_call x6 -> x7, Pallas kernels: 13 us -> 12.4 us  [the longest x4 10.2 us: products(): call(functools.partial(products_kernel, over_columns), shape_of((peers, 2...]
  transfers between devices with their start and end apart: 4 -> 4, of which waited for: 4 -> 4; matrix products, arithmetic and copies ran while one was open for 0% -> 0% of each run, Pallas kernels for 4% -> 6%
where the time goes in v4:
time: 171 us; the launch traced here: 170 us
  blocking collectives  79 us (46%)
  starting transfers between devices  33.4 us (20%)
  waiting for transfers between devices  25.6 us (15%)
  Pallas kernels  16.5 us (10%)
  local copies, waits for them, and re-layouts  13.7 us (8%)
    all_to_all x4, blocking collectives, exchange(): return lax.all_to_all(chunks, axis, split_axis=0, concat_axis=0, tiled=True)  79 us
    all_to_all x4, starting transfers between devices, exchange(): return lax.all_to_all(chunks, axis, split_axis=0, concat_axis=0, tiled=True)  33.4 us
    all_to_all x4, waiting for transfers between devices, exchange(): return lax.all_to_all(chunks, axis, split_axis=0, concat_axis=0, tiled=True)  25.6 us
    unnamed x36, local copies, waits for them, and re-layouts  13.7 us
    pallas_call x4, Pallas kernels, products(): call(functools.partial(products_kernel, over_columns), shape_of((peers, 2...  10.2 us
  transfers between devices with their start and end apart: 4, of which 4 were waited for; matrix products, arithmetic and copies ran while one was open for 0% of the time, Pallas kernels for 6%

profile of v4, /device:TPU:1, one launch (start us, length us, event | category | flops | bytes accessed | tf_op | source)
XLA Modules:
  0.0 170.4 jit_solution(9243063920560198529)
XLA Ops:
  2.0 27.7 %all_to_all.40.vectors_ref = bf16[32,16,128]{2,1,0:T(8,128)(2,1)S(1)} all-to-all(bf16[32,16,128]{2,1,0:T(8,128)(2,1)} %shard_map.104), channel_id=1, replica_groups=mesh['row'=32,'col'=32] {'row'}, dimensions={0} | all-to-all | bytes 262144 | tf_op jit(solution)/shard_map/all_to_all | solution.py:20
  29.7 11.7 %all-to-all-start.2 = ((bf16[32,16,128]{2,1,0:T(8,128)(2,1)}), bf16[32,16,128]{2,1,0:T(8,128)(2,1)S(1)}, u32[]{:S(2)}, u32[]{:S(2)}) async-start(bf16[32,16,128]{2,1,0:T(8,128)(2,1)} %shard_map.104), calls=%async_computation.2 | async-start | bytes 262144 | tf_op jit(solution)/shard_map/all_to_all | solution.py:20
  45.5 0.7 pad_add_fusion.lists_ref
  46.3 1.9 %copy-done = bf16[1,1,96,128,128]{4,3,2,1,0:T(8,128)(2,1)S(1)} copy-done((bf16[1,1,96,128,128]{4,3,2,1,0:T(8,128)(2,1)S(1)}, bf16[1,1,96,128,128]{4,3,2,1,0:T(8,128)(2,1)}, u32[]{:S(2)}) %copy-start) | copy-done | bytes 3145752
  48.2 2.9 %shard_map.105 = f32[32,2,8,128]{3,2,1,0:T(8,128)S(1)} custom-call(s32[193]{0:T(256)S(1)} %pad_add_fusion.lists_ref, bf16[32,16,128]{2,1,0:T(8,128)(2,1)S(1)} %all_to_all.40.vectors_ref, bf16[96,128,128]{2,1,0:T(8,128)(2,1)S(1)} %bitcast.6), custom_call_target="tpu_custom_call" | custom-call | tf_op jit(solution)/shard_map/pallas_call | solution.py:256
  51.8 0.9 all-to-all-done.2.vectors_ref
  52.7 10.9 %all-to-all-start.1 = ((f32[32,2,8,128]{3,2,1,0:T(8,128)}), f32[32,2,8,128]{3,2,1,0:T(8,128)S(1)}, u32[]{:S(2)}, u32[]{:S(2)}) async-start(f32[32,2,8,128]{3,2,1,0:T(8,128)} %copy-done.5), calls=%async_computation.1 | async-start | bytes 524288 | tf_op jit(solution)/shard_map/all_to_all | solution.py:20
  63.6 2.1 %shard_map.106 = f32[32,2,8,128]{3,2,1,0:T(8,128)S(1)} custom-call(s32[193]{0:T(256)S(1)} %pad_add_fusion.lists_ref, bf16[32,16,128]{2,1,0:T(8,128)(2,1)S(1)} %all-to-all-done.2.vectors_ref, bf16[96,128,128]{2,1,0:T(8,128)(2,1)S(1)} %bitcast.7), custom_call_target="tpu_custom_call" | custom-call | tf_op jit(solution)/shard_map/pallas_call | solution.py:256
  66.5 8.9 %all-to-all-done.1.near_ref = f32[32,2,8,128]{3,2,1,0:T(8,128)S(1)} async-done(((f32[32,2,8,128]{3,2,1,0:T(8,128)}), f32[32,2,8,128]{3,2,1,0:T(8,128)S(1)}, u32[]{:S(2)}, u32[]{:S(2)}) %all-to-all-start.1) | async-done | bytes 262176 | tf_op jit(solution)/shard_map/all_to_all | solution.py:20
  75.4 18.2 %all_to_all.41.far_ref = f32[32,2,8,128]{3,2,1,0:T(8,128)S(1)} all-to-all(f32[32,2,8,128]{3,2,1,0:T(8,128)} %copy-done.8), channel_id=1, replica_groups=mesh['row'=32,'col'=32] {'row'}, dimensions={0} | all-to-all | bytes 524288 | tf_op jit(solution)/shard_map/all_to_all | solution.py:20
  93.7 0.7 copy-done.12
  95.4 16.0 %all_to_all.42.vectors_ref = bf16[32,32,128]{2,1,0:T(8,128)(2,1)} all-to-all(bf16[32,32,128]{2,1,0:T(8,128)(2,1)S(1)} %get-tuple-element.15), channel_id=1, replica_groups=mesh['row'=32,'col'=32] {'row'}, dimensions={0} | all-to-all | bytes 524288 | tf_op jit(solution)/shard_map/all_to_all | solution.py:20
  111.4 4.5 %all-to-all-start.5 = ((bf16[32,32,128]{2,1,0:T(8,128)(2,1)}), bf16[32,32,128]{2,1,0:T(8,128)(2,1)S(1)}, u32[]{:S(2)}, u32[]{:S(2)}) async-start(bf16[32,32,128]{2,1,0:T(8,128)(2,1)} %copy-done.2), calls=%async_computation.5 | async-start | bytes 524288 | tf_op jit(solution)/shard_map/all_to_all | solution.py:20
  115.9 0.9 copy-done.9
  116.8 2.9 %shard_map.108.sums_ref = f32[32,2,8,128]{3,2,1,0:T(8,128)S(1)} custom-call(s32[193]{0:T(256)S(1)} %pad_add_fusion.lists_ref, bf16[32,32,128]{2,1,0:T(8,128)(2,1)S(1)} %copy-done.9, bf16[96,128,128]{2,1,0:T(8,128)(2,1)S(1)} %bitcast.8), custom_call_target="tpu_custom_call" | custom-call | tf_op jit(solution)/shard_map/pallas_call | solution.py:256
  120.5 7.1 %all-to-all-done.5.near_ref.vectors_ref = bf16[32,32,128]{2,1,0:T(8,128)(2,1)S(1)} async-done(((bf16[32,32,128]{2,1,0:T(8,128)(2,1)}), bf16[32,32,128]{2,1,0:T(8,128)(2,1)S(1)}, u32[]{:S(2)}, u32[]{:S(2)}) %all-to-all-start.5) | async-done | bytes 262176 | tf_op jit(solution)/shard_map/all_to_all | solution.py:20
  127.6 0.9 copy-done.4
  130.0 6.3 %all-to-all-start.6 = ((bf16[32,24,128]{2,1,0:T(8,128)(2,1)}), bf16[32,24,128]{2,1,0:T(8,128)(2,1)}, u32[]{:S(2)}, u32[]{:S(2)}) async-start(bf16[32,24,128]{2,1,0:T(8,128)(2,1)} %copy-done.10), calls=%async_computation.6 | async-start | bytes 393216 | tf_op jit(solution)/shard_map/all_to_all | solution.py:20
  136.3 2.1 %shard_map.110.far_ref = f32[32,2,8,128]{3,2,1,0:T(8,128)S(1)} custom-call(s32[193]{0:T(256)S(1)} %pad_add_fusion.lists_ref, bf16[32,32,128]{2,1,0:T(8,128)(2,1)S(1)} %all-to-all-done.5.near_ref.vectors_ref, bf16[96,128,128]{2,1,0:T(8,128)(2,1)S(1)} %bitcast.9), custom_call_target="tpu_custom_call" | custom-call | tf_op jit(solution)/shard_map/pallas_call | solution.py:256
  139.1 8.6 %all-to-all-done.6.near_ref = bf16[32,24,128]{2,1,0:T(8,128)(2,1)} async-done(((bf16[32,24,128]{2,1,0:T(8,128)(2,1)}), bf16[32,24,128]{2,1,0:T(8,128)(2,1)}, u32[]{:S(2)}, u32[]{:S(2)}) %all-to-all-start.6) | async-done | bytes 196640 | tf_op jit(solution)/shard_map/all_to_all | solution.py:20
  147.8 0.9 copy-done.7
  148.7 1.3 shard_map.111
  150.0 17.0 %all_to_all.43.far_ref = bf16[32,24,128]{2,1,0:T(8,128)(2,1)S(1)} all-to-all(bf16[32,24,128]{2,1,0:T(8,128)(2,1)S(1)} %get-tuple-element.17), channel_id=1, replica_groups=mesh['row'=32,'col'=32] {'row'}, dimensions={0} | all-to-all | bytes 393216 | tf_op jit(solution)/shard_map/all_to_all | solution.py:20
  167.0 3.4 %shard_map.112 = (f32[8,256]{1,0:T(8,128)}, f32[8,256]{1,0:T(8,128)}, f32[3,8,8]{2,1,0:T(8,128)}) custom-call(bf16[32,24,128]{2,1,0:T(8,128)(2,1)S(1)} %all_to_all.43.far_ref, f32[32,256]{1,0:T(8,128)S(1)} %get-tuple-element.18.state_ref), custom_call_target="tpu_custom_call" | custom-call | tf_op jit(solution)/shard_map/pallas_call | solution.py:293
  (35 shorter events, 9.9 us)
Async XLA Ops:
  0.6 0.7 copy-start.13
  29.7 22.9 %all-to-all-start.2 = ((bf16[32,16,128]{2,1,0:T(8,128)(2,1)}), bf16[32,16,128]{2,1,0:T(8,128)(2,1)S(1)}, u32[]{:S(2)}, u32[]{:S(2)}) async-start(bf16[32,16,128]{2,1,0:T(8,128)(2,1)} %shard_map.104), calls=%async_computation.2 | async-start | bytes 262144 | tf_op jit(solution)/shard_map/all_to_all | solution.py:20
  42.1 0.7 copy-start.14
  42.8 0.7 copy-start.15
  43.5 0.7 copy-start.16
  44.2 0.7 copy-start.17
  44.9 0.6 copy-start.11
  46.3 1.9 %copy-start = (bf16[1,1,96,128,128]{4,3,2,1,0:T(8,128)(2,1)S(1)}, bf16[1,1,96,128,128]{4,3,2,1,0:T(8,128)(2,1)}, u32[]{:S(2)}) copy-start(bf16[1,1,96,128,128]{4,3,2,1,0:T(8,128)(2,1)} %param.12) | copy-start | bytes 9437188
  48.2 15.5 %copy-start.1 = (bf16[1,1,96,128,128]{4,3,2,1,0:T(8,128)(2,1)S(1)}, bf16[1,1,96,128,128]{4,3,2,1,0:T(8,128)(2,1)}, u32[]{:S(2)}) copy-start(bf16[1,1,96,128,128]{4,3,2,1,0:T(8,128)(2,1)} %param.12) | copy-start | bytes 9437188
  51.1 0.7 copy-start.5
  52.7 22.7 %all-to-all-start.1 = ((f32[32,2,8,128]{3,2,1,0:T(8,128)}), f32[32,2,8,128]{3,2,1,0:T(8,128)S(1)}, u32[]{:S(2)}, u32[]{:S(2)}) async-start(f32[32,2,8,128]{3,2,1,0:T(8,128)} %copy-done.5), calls=%async_computation.1 | async-start | bytes 524288 | tf_op jit(solution)/shard_map/all_to_all | solution.py:20
  65.8 0.7 copy-start.8
  93.7 0.7 copy-start.12
  94.7 0.7 copy-start.2
  111.4 16.2 %all-to-all-start.5 = ((bf16[32,32,128]{2,1,0:T(8,128)(2,1)}), bf16[32,32,128]{2,1,0:T(8,128)(2,1)S(1)}, u32[]{:S(2)}, u32[]{:S(2)}) async-start(bf16[32,32,128]{2,1,0:T(8,128)(2,1)} %copy-done.2), calls=%async_computation.5 | async-start | bytes 524288 | tf_op jit(solution)/shard_map/all_to_all | solution.py:20
  115.9 1.0 copy-start.9
  119.8 0.7 copy-start.3
  127.6 1.0 copy-start.4
  129.3 0.7 copy-start.10
  130.0 17.8 %all-to-all-start.6 = ((bf16[32,24,128]{2,1,0:T(8,128)(2,1)}), bf16[32,24,128]{2,1,0:T(8,128)(2,1)}, u32[]{:S(2)}, u32[]{:S(2)}) async-start(bf16[32,24,128]{2,1,0:T(8,128)(2,1)} %copy-done.10), calls=%async_computation.6 | async-start | bytes 393216 | tf_op jit(solution)/shard_map/all_to_all | solution.py:20
  138.4 0.7 copy-start.6
  147.8 1.0 copy-start.7

commit v5 on v4

--- a/solution.py
+++ b/solution.py
@@ -84,39 +84,68 @@
     out_ref[...] = jnp.broadcast_to(chunk[None], out_ref.shape)
 
 
-def pack_kernel(current_ref, previous_ref, beta_ref, diagonal_ref, out_ref):
+def pack_kernel(
+    current_ref, previous_ref, beta_ref, diagonal_ref, blocks_ref, out_ref, held_ref
+):
     nv = current_ref.shape[0]
+    held_ref[...] = blocks_ref[...]
     out_ref[:nv] = current_ref[...]
     out_ref[nv : 2 * nv] = small_dot(beta_ref[...], previous_ref[...])
     out_ref[2 * nv :] = jnp.broadcast_to(diagonal_ref[...], (nv, out_ref.shape[1]))
 
 
-def products_kernel(over_columns, lists_ref, vectors_ref, blocks_ref, out_ref, products_ref):
+def place_products(
+    lists_ref, near_ref, far_ref, blocks_ref, near_out, far_out, near_products, far_products
+):
     slots = blocks_ref.shape[0]
-    src, dst = (slots, 0) if over_columns else (0, slots)
-    nv = out_ref.shape[2]
-    has_low = vectors_ref.shape[1] > 2 * nv
-    dims = (((1,), (1 if over_columns else 0,)), ((), ()))
+    nv = near_out.shape[2]
+
+    def product(ref, index, block, block_dim):
+        pair = ref[lax.shift_right_logical(index, 1)]
+        values = lax.dot_general(
+            pair, block, (((1,), (block_dim,)), ((), ())), preferred_element_type=F32
+        )
+        if ref.shape[1] > 2 * nv:
+            values = values[: 2 * nv] + values[2 * nv :]
+        return values
+
     for k in range(slots):
-        pair = vectors_ref[lax.shift_right_logical(lists_ref[src + k], 1)]
-        product = lax.dot_general(pair, blocks_ref[k], dims, preferred_element_type=F32)
-        if has_low:
-            product = product[: 2 * nv] + product[2 * nv :]
-        products_ref[k] = product
-    out_ref[...] = jnp.zeros_like(out_ref)
+        block = blocks_ref[k]
+        near_products[k] = product(far_ref, lists_ref[slots + k], block, 1)
+        far_products[k] = product(near_ref, lists_ref[k], block, 0)
+    near_out[...] = jnp.zeros_like(near_out)
+    far_out[...] = jnp.zeros_like(far_out)
 
     def one_slot(k, carry):
-        half = pl.multiple_of((lists_ref[src + k] & 1) * nv, nv)
-        block = lists_ref[dst + k]
-        out_ref[lax.shift_right_logical(block, 1), block & 1] += products_ref[
-            k, pl.ds(half, nv), :
+        near, far = lists_ref[k], lists_ref[slots + k]
+        near_half, far_half = near & 1, far & 1
+        near_chunk, far_chunk = lax.shift_right_logical(near, 1), lax.shift_right_logical(far, 1)
+        near_out[near_chunk, near_half] += near_products[
+            k, pl.ds(pl.multiple_of(far_half * nv, nv), nv), :
+        ]
+        far_out[far_chunk, far_half] += far_products[
+            k, pl.ds(pl.multiple_of(near_half * nv, nv), nv), :
         ]
         return carry
 
     lax.fori_loop(0, lists_ref[2 * slots], one_slot, 0)
 
 
-def quadratic_kernel(sums_ref, near_ref, state_ref, out_ref):
+def second_kernel(
+    lists_ref,
+    near_ref,
+    far_ref,
+    blocks_ref,
+    state_ref,
+    out_ref,
+    far_out,
+    near_products,
+    far_products,
+    sums_ref,
+):
+    place_products(
+        lists_ref, near_ref, far_ref, blocks_ref, sums_ref, far_out, near_products, far_products
+    )
     nv, width = sums_ref.shape[2:]
     total = jnp.zeros((4 * nv, 4 * nv), F32)
     for n in range(out_ref.shape[0]):
@@ -251,24 +280,23 @@
     slots, width = tile_blocks.shape[:2]
     n_row, n_col = lax.axis_size("row"), lax.axis_size("col")
     rows_total = share * n_row * n_col
-
-    def products(over_columns, vectors, peers):
-        return call(
-            functools.partial(products_kernel, over_columns),
-            shape_of((peers, 2, nv, width)),
-            [SMEM, VMEM, VMEM],
-            [pltpu.VMEM((slots, 2 * nv, width), F32)],
-        )(lists, vectors, tile_blocks)
+    near_sums, far_sums = (n_col, 2, nv, width), (n_row, 2, nv, width)
+    products_scratch = [pltpu.VMEM((slots, 2 * nv, width), F32)] * 2
 
     chunks = call(rounded_kernel, shape_of((n_col, 2 * nv, width), BF16), [VMEM])(current_block)
-    constants = call(pack_kernel, shape_of((3 * nv, share)), [VMEM] * 4)(
-        current_block, previous_block, beta_coupling, diagonal.reshape(1, share)
-    )
-    lists, constants = lax.optimization_barrier((lists, constants))
+    constants, held_blocks = call(
+        pack_kernel, (shape_of((3 * nv, share)), shape_of(tile_blocks.shape, BF16)), [VMEM] * 5
+    )(current_block, previous_block, beta_coupling, diagonal.reshape(1, share), tile_blocks)
     near_vectors = exchange(chunks, "col")
     far_vectors = exchange(chunks, "row")
-    far_got = exchange(products(False, near_vectors, n_row), "row")
-    near_got = exchange(products(True, far_vectors, n_col), "col")
+    near_part, far_part = call(
+        place_products,
+        (shape_of(near_sums), shape_of(far_sums)),
+        [SMEM, VMEM, VMEM, VMEM],
+        products_scratch,
+    )(lists, near_vectors, far_vectors, held_blocks)
+    far_got = exchange(far_part, "row")
+    near_got = exchange(near_part, "col")
     state, chunks = call(
         middle_kernel,
         (shape_of((5 * nv, share)), shape_of((n_col, 4 * nv, width), BF16)),
@@ -276,14 +304,14 @@
     )(near_got, far_got, constants)
 
     far_vectors = exchange(chunks, "row")
-    chunks, far_vectors = lax.optimization_barrier((chunks, far_vectors))
     near_vectors = exchange(chunks, "col")
-    near_part = products(True, far_vectors, n_col)
-    near_part = call(quadratic_kernel, shape_of((n_col, 3 * nv, width), BF16), [VMEM] * 3)(
-        near_part, near_vectors, state
-    )
+    near_part, far_part = call(
+        second_kernel,
+        (shape_of((n_col, 3 * nv, width), BF16), shape_of(far_sums)),
+        [SMEM, VMEM, VMEM, VMEM, VMEM],
+        products_scratch + [pltpu.VMEM(near_sums, F32)],
+    )(lists, near_vectors, far_vectors, held_blocks, state)
     near_got = exchange(near_part, "col")
-    far_part = products(False, near_vectors, n_row)
     late, far_part = call(
         forward_kernel,
         (shape_of((4 * nv, share)), shape_of((n_row, 3 * nv, width), BF16)),

time: 171 us -> 167 us (0.977)
  blocking collectives: 79 us -> 129 us
  starting transfers between devices: 33.4 us -> 11.7 us
  waiting for transfers between devices: 25.6 us -> 5.63 us
  local copies, waits for them, and re-layouts: 13.7 us -> 5.34 us
  Pallas kernels: 16.5 us -> 13.6 us
    all_to_all x4 -> x7, blocking collectives: 79 us -> 129 us  [exchange(): return lax.all_to_all(chunks, axis, split_axis=0, concat_axis=0, tiled=True)]
    all_to_all x4 -> x1, starting transfers between devices: 33.4 us -> 11.7 us  [exchange(): return lax.all_to_all(chunks, axis, split_axis=0, concat_axis=0, tiled=True)]
    all_to_all x4 -> x1, waiting for transfers between devices: 25.6 us -> 5.63 us  [exchange(): return lax.all_to_all(chunks, axis, split_axis=0, concat_axis=0, tiled=True)]
    unnamed x36 -> x16, local copies, waits for them, and re-layouts: 13.7 us -> 5.34 us
    pallas_call x6 -> x3, Pallas kernels: 11 us -> 8.98 us  [the longest x1 4.86 us: on_device(): call(second_kernel, (shape_of((n_col, 3 * nv, width), BF16), shape_of(far...]
  transfers between devices with their start and end apart: 4 -> 1, of which waited for: 4 -> 1; matrix products, arithmetic and copies ran while one was open for 0% -> 0% of each run, Pallas kernels for 6% -> 0%
where the time goes in v5:
time: 167 us
  blocking collectives  129 us (77%)
  Pallas kernels  13.6 us (8%)
  starting transfers between devices  11.7 us (7%)
  waiting for transfers between devices  5.63 us (3%)
  local copies, waits for them, and re-layouts  5.34 us (3%)
    all_to_all x7, blocking collectives, exchange(): return lax.all_to_all(chunks, axis, split_axis=0, concat_axis=0, tiled=True)  129 us
    all_to_all x1, starting transfers between devices, exchange(): return lax.all_to_all(chunks, axis, split_axis=0, concat_axis=0, tiled=True)  11.7 us
    all_to_all x1, waiting for transfers between devices, exchange(): return lax.all_to_all(chunks, axis, split_axis=0, concat_axis=0, tiled=True)  5.63 us
    unnamed x16, local copies, waits for them, and re-layouts  5.34 us
    pallas_call x1, Pallas kernels, on_device(): call(second_kernel, (shape_of((n_col, 3 * nv, width), BF16), shape_of(far...  4.86 us
    pallas_call x1, Pallas kernels, on_device(): call(place_products, (shape_of(near_sums), shape_of(far_sums)), [SMEM, VM...  3.9 us
    pallas_call x1, Pallas kernels, on_device(): call(functools.partial(last_kernel, rows_total), (shape_of((nv, share)),...  3.38 us
  transfers between devices with their start and end apart: 1, of which 1 were waited for; matrix products, arithmetic and copies ran while one was open for 0% of the time, Pallas kernels for 0%

profile of v5, /device:TPU:1, one launch (start us, length us, event | category | flops | bytes accessed | tf_op | source)
XLA Modules:
  0.0 166.6 jit_solution(10570674666488317316)
XLA Ops:
  0.6 0.0 copy-start.1
  0.6 0.7 copy-done.1
  1.3 0.7 shard_map.103
  2.0 27.7 %all_to_all.40.far_ref = bf16[32,16,128]{2,1,0:T(8,128)(2,1)S(1)} all-to-all(bf16[32,16,128]{2,1,0:T(8,128)(2,1)} %shard_map.103), channel_id=1, replica_groups=mesh['row'=32,'col'=32] {'row'}, dimensions={0} | all-to-all | bytes 262144 | tf_op jit(solution)/shard_map/all_to_all | solution.py:20
  29.7 11.7 %all-to-all-start = ((bf16[32,16,128]{2,1,0:T(8,128)(2,1)}), bf16[32,16,128]{2,1,0:T(8,128)(2,1)S(1)}, u32[]{:S(2)}, u32[]{:S(2)}) async-start(bf16[32,16,128]{2,1,0:T(8,128)(2,1)} %shard_map.103), calls=%async_computation | async-start | bytes 262144 | tf_op jit(solution)/shard_map/all_to_all | solution.py:20
  42.1 1.9 %copy-done = bf16[1,1,96,128,128]{4,3,2,1,0:T(8,128)(2,1)S(1)} copy-done((bf16[1,1,96,128,128]{4,3,2,1,0:T(8,128)(2,1)S(1)}, bf16[1,1,96,128,128]{4,3,2,1,0:T(8,128)(2,1)}, u32[]{:S(2)}) %copy-start) | copy-done | bytes 3145752
  44.0 0.7 copy-done.2
  44.7 0.7 copy-done.3
  45.4 0.7 copy-done.4
  46.1 0.7 copy-done.5
  46.7 0.2 shard_map.104
  47.0 0.1 pad_add_fusion.lists_ref
  47.0 5.6 %all-to-all-done.near_ref = bf16[32,16,128]{2,1,0:T(8,128)(2,1)S(1)} async-done(((bf16[32,16,128]{2,1,0:T(8,128)(2,1)}), bf16[32,16,128]{2,1,0:T(8,128)(2,1)S(1)}, u32[]{:S(2)}, u32[]{:S(2)}) %all-to-all-start) | async-done | bytes 131104 | tf_op jit(solution)/shard_map/all_to_all | solution.py:20
  52.7 3.9 %shard_map.105 = (f32[32,2,8,128]{3,2,1,0:T(8,128)S(1)}, f32[32,2,8,128]{3,2,1,0:T(8,128)S(1)}) custom-call(s32[193]{0:T(256)S(1)} %pad_add_fusion.lists_ref, bf16[32,16,128]{2,1,0:T(8,128)(2,1)S(1)} %all-to-all-done.near_ref, bf16[32,16,128]{2,1,0:T(8,128)(2,1)S(1)} %all_to_all.40.far_ref, bf16[96,128,128]{2,1,0:T(8,128)(2,1)S(1)} %get-tuple-element.13.blocks_ref), custom_call_target="tpu_custom_call" | custom-call | tf_op jit(solution)/shard_map/pallas_call | solution.py:292
  56.6 17.3 %all_to_all.41.near_ref = f32[32,2,8,128]{3,2,1,0:T(8,128)S(1)} all-to-all(f32[32,2,8,128]{3,2,1,0:T(8,128)S(1)} %get-tuple-element.14), channel_id=1, replica_groups=mesh['row'=32,'col'=32] {'col'}, dimensions={0} | all-to-all | bytes 524288 | tf_op jit(solution)/shard_map/all_to_all | solution.py:20
  73.9 18.7 %all_to_all.42.far_ref = f32[32,2,8,128]{3,2,1,0:T(8,128)S(1)} all-to-all(f32[32,2,8,128]{3,2,1,0:T(8,128)S(1)} %get-tuple-element.15), channel_id=1, replica_groups=mesh['row'=32,'col'=32] {'row'}, dimensions={0} | all-to-all | bytes 524288 | tf_op jit(solution)/shard_map/all_to_all | solution.py:20
  92.6 0.3 shard_map.106
  92.9 15.4 %all_to_all.43.far_ref = bf16[32,32,128]{2,1,0:T(8,128)(2,1)S(1)} all-to-all(bf16[32,32,128]{2,1,0:T(8,128)(2,1)S(1)} %get-tuple-element.17), channel_id=1, replica_groups=mesh['row'=32,'col'=32] {'row'}, dimensions={0} | all-to-all | bytes 524288 | tf_op jit(solution)/shard_map/all_to_all | solution.py:20
  108.3 15.6 %all_to_all.44.near_ref = bf16[32,32,128]{2,1,0:T(8,128)(2,1)S(1)} all-to-all(bf16[32,32,128]{2,1,0:T(8,128)(2,1)S(1)} %get-tuple-element.17), channel_id=1, replica_groups=mesh['row'=32,'col'=32] {'col'}, dimensions={0} | all-to-all | bytes 524288 | tf_op jit(solution)/shard_map/all_to_all | solution.py:20
  123.9 4.9 %shard_map.107 = (bf16[32,24,128]{2,1,0:T(8,128)(2,1)S(1)}, f32[32,2,8,128]{3,2,1,0:T(8,128)S(1)}) custom-call(s32[193]{0:T(256)S(1)} %pad_add_fusion.lists_ref, bf16[32,32,128]{2,1,0:T(8,128)(2,1)S(1)} %all_to_all.44.near_ref, bf16[32,32,128]{2,1,0:T(8,128)(2,1)S(1)} %all_to_all.43.far_ref, bf16[96,128,128]{2,1,0:T(8,128)(2,1)S(1)} %get-tuple-element.13.blocks_ref, ...), custom_call_target="tpu_custom_call" | custom-call | tf_op jit(solution)/shard_map/pallas_call | solution.py:308
  128.8 18.3 %all_to_all.45.near_ref = bf16[32,24,128]{2,1,0:T(8,128)(2,1)S(1)} all-to-all(bf16[32,24,128]{2,1,0:T(8,128)(2,1)S(1)} %get-tuple-element.19), channel_id=1, replica_groups=mesh['row'=32,'col'=32] {'col'}, dimensions={0} | all-to-all | bytes 393216 | tf_op jit(solution)/shard_map/all_to_all | solution.py:20
  147.0 0.3 shard_map.108
  147.3 15.9 %all_to_all.46.far_ref = bf16[32,24,128]{2,1,0:T(8,128)(2,1)S(1)} all-to-all(bf16[32,24,128]{2,1,0:T(8,128)(2,1)S(1)} %get-tuple-element.21), channel_id=1, replica_groups=mesh['row'=32,'col'=32] {'row'}, dimensions={0} | all-to-all | bytes 393216 | tf_op jit(solution)/shard_map/all_to_all | solution.py:20
  163.2 3.4 %shard_map.109 = (f32[8,256]{1,0:T(8,128)}, f32[8,256]{1,0:T(8,128)}, f32[3,8,8]{2,1,0:T(8,128)}) custom-call(bf16[32,24,128]{2,1,0:T(8,128)(2,1)S(1)} %all_to_all.46.far_ref, f32[32,256]{1,0:T(8,128)S(1)} %get-tuple-element.22.state_ref), custom_call_target="tpu_custom_call" | custom-call | tf_op jit(solution)/shard_map/pallas_call | solution.py:321
  (9 shorter events, 0.0 us)
Async XLA Ops:
  0.6 0.7 copy-start.1
  1.3 45.6 %copy-start.6 = (s32[1,1,96]{2,1,0:T(1,128)S(1)}, s32[1,1,96]{2,1,0:T(1,128)}, u32[]{:S(2)}) copy-start(s32[1,1,96]{2,1,0:T(1,128)} %param.14) | copy-start | bytes 1156
  1.3 45.6 %copy-start.7 = (s32[1,1,96]{2,1,0:T(1,128)S(1)}, s32[1,1,96]{2,1,0:T(1,128)}, u32[]{:S(2)}) copy-start(s32[1,1,96]{2,1,0:T(1,128)} %param.13) | copy-start | bytes 1156
  29.7 22.9 %all-to-all-start = ((bf16[32,16,128]{2,1,0:T(8,128)(2,1)}), bf16[32,16,128]{2,1,0:T(8,128)(2,1)S(1)}, u32[]{:S(2)}, u32[]{:S(2)}) async-start(bf16[32,16,128]{2,1,0:T(8,128)(2,1)} %shard_map.103), calls=%async_computation | async-start | bytes 262144 | tf_op jit(solution)/shard_map/all_to_all | solution.py:20
  42.1 1.9 %copy-start = (bf16[1,1,96,128,128]{4,3,2,1,0:T(8,128)(2,1)S(1)}, bf16[1,1,96,128,128]{4,3,2,1,0:T(8,128)(2,1)}, u32[]{:S(2)}) copy-start(bf16[1,1,96,128,128]{4,3,2,1,0:T(8,128)(2,1)} %param.12) | copy-start | bytes 9437188
  44.0 0.7 copy-start.2
  44.7 0.7 copy-start.3
  45.4 0.7 copy-start.4
  46.0 0.7 copy-start.5

commit v6 on v5

--- a/solution.py
+++ b/solution.py
@@ -52,6 +52,12 @@
     for k in range(1, right.shape[0]):
         total = total + left[:, k : k + 1] * right[k : k + 1, :]
     return total
+
+
+def transposed(matrix):
+    size = matrix.shape[0]
+    tile = jnp.concatenate([matrix, jnp.zeros((size, 128 - size), F32)], axis=1)
+    return jnp.transpose(tile)[:size]
 
 
 def identity(size):
@@ -129,6 +135,26 @@
         return carry
 
     lax.fori_loop(0, lists_ref[2 * slots], one_slot, 0)
+
+
+def first_kernel(
+    lists_ref,
+    near_ref,
+    far_ref,
+    blocks_ref,
+    near_out,
+    far_out,
+    near_products,
+    far_products,
+    near_sums,
+    far_sums,
+):
+    place_products(
+        lists_ref, near_ref, far_ref, blocks_ref, near_sums, far_sums, near_products, far_products
+    )
+    for out_ref, sums_ref in ((near_out, near_sums), (far_out, far_sums)):
+        for n in range(out_ref.shape[0]):
+            out_ref[n] = jnp.concatenate([sums_ref[n, 0], sums_ref[n, 1]], axis=0).astype(BF16)
 
 
 def second_kernel(
@@ -169,15 +195,15 @@
 
 
 def middle_kernel(near_ref, far_ref, constants_ref, state_ref, payload_ref):
-    nv, width = near_ref.shape[2:]
+    nv, width = near_ref.shape[1] // 2, near_ref.shape[2]
+    off = jnp.sum(near_ref[...].astype(F32), axis=0) + jnp.sum(far_ref[...].astype(F32), axis=0)
     total = jnp.zeros((3 * nv, 3 * nv), F32)
     halves = []
     for t in range(2):
         part = slice(t * width, (t + 1) * width)
         current = constants_ref[:nv, part]
         diag = constants_ref[2 * nv :, part]
-        off_diagonal = jnp.sum(near_ref[:, t], axis=0) + jnp.sum(far_ref[:, t], axis=0)
-        applied = off_diagonal + diag * current
+        applied = off[t * nv : (t + 1) * nv] + diag * current
         shifted = applied - constants_ref[nv : 2 * nv, part] - SHIFT * current
         stack = jnp.concatenate([current, shifted, applied], axis=0)
         state_ref[: 3 * nv, part] = stack
@@ -223,7 +249,7 @@
     gram = lambda i: extra[:, i * nv : (i + 1) * nv]
     cc, xx, cx, xu, cu, xw = (gram(i) for i in range(6))
     eye = identity(nv)
-    xc = contract_last(eye, cx)
+    xc = transposed(cx)
     scale = 1.0 / rows_total
     alpha_one = (cx + SHIFT * cc) * scale
     alpha = alpha_one - SHIFT * eye
@@ -235,6 +261,7 @@
     factor = jnp.zeros((nv, nv), F32)
     factor_t = jnp.zeros((nv, nv), F32)
     inverse = eye
+    inverse_t = eye
     for j in range(nv):
         root = lax.rsqrt(work[j : j + 1, j : j + 1])
         column = jnp.where(rows[:, :1] >= j, work[:, j : j + 1] * root, 0.0)
@@ -245,16 +272,19 @@
         done = inverse[j : j + 1, :] * root
         below = jnp.where(rows[:, :1] > j, column, 0.0)
         inverse = jnp.where(rows == j, done, inverse - below * done)
+        done_t = inverse_t[:, j : j + 1] * root
+        right = jnp.where(columns[:1] > j, row, 0.0)
+        inverse_t = jnp.where(columns == j, done_t, inverse_t - done_t * right)
     half = small_dot(xu, alpha)
     z = (
         xw
         - half
-        - contract_last(eye, half)
+        - transposed(half)
         + small_dot(small_dot(alpha_t, cu), alpha)
     )
-    alpha_two = contract_last(small_dot(inverse, z), inverse)
+    alpha_two = small_dot(small_dot(inverse, z), inverse_t)
     alpha_two = (alpha_two - small_dot(small_dot(inverse, adjusted_c), factor)) * scale
-    alpha_two_t = contract_last(eye, alpha_two)
+    alpha_two_t = transposed(alpha_two)
     for t in range(2):
         part = slice(t * width, (t + 1) * width)
         current = state_ref[:nv, part]
@@ -290,10 +320,10 @@
     near_vectors = exchange(chunks, "col")
     far_vectors = exchange(chunks, "row")
     near_part, far_part = call(
-        place_products,
-        (shape_of(near_sums), shape_of(far_sums)),
+        first_kernel,
+        (shape_of((n_col, 2 * nv, width), BF16), shape_of((n_row, 2 * nv, width), BF16)),
         [SMEM, VMEM, VMEM, VMEM],
-        products_scratch,
+        products_scratch + [pltpu.VMEM(near_sums, F32), pltpu.VMEM(far_sums, F32)],
     )(lists, near_vectors, far_vectors, held_blocks)
     far_got = exchange(far_part, "row")
     near_got = exchange(near_part, "col")

time: 167 us -> 162 us (0.970)
  blocking collectives: 129 us -> 124 us
    all_to_all x7, blocking collectives: 129 us -> 124 us  [exchange(): return lax.all_to_all(chunks, axis, split_axis=0, concat_axis=0, tiled=True)]
where the time goes in v6:
time: 162 us; the launch traced here: 161 us
  blocking collectives  124 us (77%)
  Pallas kernels  12.9 us (8%)
  starting transfers between devices  11.7 us (7%)
  waiting for transfers between devices  5.63 us (3%)
  local copies, waits for them, and re-layouts  5.34 us (3%)
    all_to_all x7, blocking collectives, exchange(): return lax.all_to_all(chunks, axis, split_axis=0, concat_axis=0, tiled=True)  124 us
    all_to_all x1, starting transfers between devices, exchange(): return lax.all_to_all(chunks, axis, split_axis=0, concat_axis=0, tiled=True)  11.7 us
    all_to_all x1, waiting for transfers between devices, exchange(): return lax.all_to_all(chunks, axis, split_axis=0, concat_axis=0, tiled=True)  5.63 us
    unnamed x16, local copies, waits for them, and re-layouts  5.34 us
    pallas_call x1, Pallas kernels, on_device(): call(second_kernel, (shape_of((n_col, 3 * nv, width), BF16), shape_of(far...  4.58 us
    pallas_call x1, Pallas kernels, on_device(): call(first_kernel, (shape_of((n_col, 2 * nv, width), BF16), shape_of((n_r...  3.66 us
  transfers between devices with their start and end apart: 1, of which 1 were waited for; matrix products, arithmetic and copies ran while one was open for 0% of the time, Pallas kernels for 0%

profile of v6, /device:TPU:1, one launch (start us, length us, event | category | flops | bytes accessed | tf_op | source)
XLA Modules:
  0.0 161.3 jit_solution(4119779838538016144)
XLA Ops:
  0.6 0.0 copy-start.1
  0.6 0.7 copy-done.1
  1.3 0.7 shard_map.103
  2.0 27.7 %all_to_all.40.far_ref = bf16[32,16,128]{2,1,0:T(8,128)(2,1)S(1)} all-to-all(bf16[32,16,128]{2,1,0:T(8,128)(2,1)} %shard_map.103), channel_id=1, replica_groups=mesh['row'=32,'col'=32] {'row'}, dimensions={0} | all-to-all | bytes 262144 | tf_op jit(solution)/shard_map/all_to_all | solution.py:20
  29.7 11.7 %all-to-all-start = ((bf16[32,16,128]{2,1,0:T(8,128)(2,1)}), bf16[32,16,128]{2,1,0:T(8,128)(2,1)S(1)}, u32[]{:S(2)}, u32[]{:S(2)}) async-start(bf16[32,16,128]{2,1,0:T(8,128)(2,1)} %shard_map.103), calls=%async_computation | async-start | bytes 262144 | tf_op jit(solution)/shard_map/all_to_all | solution.py:20
  42.1 1.9 %copy-done = bf16[1,1,96,128,128]{4,3,2,1,0:T(8,128)(2,1)S(1)} copy-done((bf16[1,1,96,128,128]{4,3,2,1,0:T(8,128)(2,1)S(1)}, bf16[1,1,96,128,128]{4,3,2,1,0:T(8,128)(2,1)}, u32[]{:S(2)}) %copy-start) | copy-done | bytes 3145752
  44.0 0.7 copy-done.2
  44.7 0.7 copy-done.3
  45.4 0.7 copy-done.4
  46.1 0.7 copy-done.5
  46.7 0.2 shard_map.104
  47.0 0.1 pad_add_fusion.lists_ref
  47.0 5.6 %all-to-all-done.near_ref = bf16[32,16,128]{2,1,0:T(8,128)(2,1)S(1)} async-done(((bf16[32,16,128]{2,1,0:T(8,128)(2,1)}), bf16[32,16,128]{2,1,0:T(8,128)(2,1)S(1)}, u32[]{:S(2)}, u32[]{:S(2)}) %all-to-all-start) | async-done | bytes 131104 | tf_op jit(solution)/shard_map/all_to_all | solution.py:20
  52.7 3.7 %shard_map.105 = (bf16[32,16,128]{2,1,0:T(8,128)(2,1)S(1)}, bf16[32,16,128]{2,1,0:T(8,128)(2,1)S(1)}) custom-call(s32[193]{0:T(256)S(1)} %pad_add_fusion.lists_ref, bf16[32,16,128]{2,1,0:T(8,128)(2,1)S(1)} %all-to-all-done.near_ref, bf16[32,16,128]{2,1,0:T(8,128)(2,1)S(1)} %all_to_all.40.far_ref, bf16[96,128,128]{2,1,0:T(8,128)(2,1)S(1)} %get-tuple-element.13.blocks_ref), custom_call_target="tpu_custom_call" | custom-call | tf_op jit(solution)/shard_map/pallas_call | solution.py:322
  56.3 17.2 %all_to_all.41.near_ref = bf16[32,16,128]{2,1,0:T(8,128)(2,1)S(1)} all-to-all(bf16[32,16,128]{2,1,0:T(8,128)(2,1)S(1)} %get-tuple-element.14), channel_id=1, replica_groups=mesh['row'=32,'col'=32] {'col'}, dimensions={0} | all-to-all | bytes 262144 | tf_op jit(solution)/shard_map/all_to_all | solution.py:20
  73.5 15.0 %all_to_all.42.far_ref = bf16[32,16,128]{2,1,0:T(8,128)(2,1)S(1)} all-to-all(bf16[32,16,128]{2,1,0:T(8,128)(2,1)S(1)} %get-tuple-element.15), channel_id=1, replica_groups=mesh['row'=32,'col'=32] {'row'}, dimensions={0} | all-to-all | bytes 262144 | tf_op jit(solution)/shard_map/all_to_all | solution.py:20
  88.5 0.3 shard_map.106
  88.7 15.2 %all_to_all.43.far_ref = bf16[32,32,128]{2,1,0:T(8,128)(2,1)S(1)} all-to-all(bf16[32,32,128]{2,1,0:T(8,128)(2,1)S(1)} %get-tuple-element.17), channel_id=1, replica_groups=mesh['row'=32,'col'=32] {'row'}, dimensions={0} | all-to-all | bytes 524288 | tf_op jit(solution)/shard_map/all_to_all | solution.py:20
  104.0 14.7 %all_to_all.44.near_ref = bf16[32,32,128]{2,1,0:T(8,128)(2,1)S(1)} all-to-all(bf16[32,32,128]{2,1,0:T(8,128)(2,1)S(1)} %get-tuple-element.17), channel_id=1, replica_groups=mesh['row'=32,'col'=32] {'col'}, dimensions={0} | all-to-all | bytes 524288 | tf_op jit(solution)/shard_map/all_to_all | solution.py:20
  118.7 4.6 %shard_map.107 = (bf16[32,24,128]{2,1,0:T(8,128)(2,1)S(1)}, f32[32,2,8,128]{3,2,1,0:T(8,128)S(1)}) custom-call(s32[193]{0:T(256)S(1)} %pad_add_fusion.lists_ref, bf16[32,32,128]{2,1,0:T(8,128)(2,1)S(1)} %all_to_all.44.near_ref, bf16[32,32,128]{2,1,0:T(8,128)(2,1)S(1)} %all_to_all.43.far_ref, bf16[96,128,128]{2,1,0:T(8,128)(2,1)S(1)} %get-tuple-element.13.blocks_ref, ...), custom_call_target="tpu_custom_call" | custom-call | tf_op jit(solution)/shard_map/pallas_call | solution.py:338
  123.3 18.5 %all_to_all.45.near_ref = bf16[32,24,128]{2,1,0:T(8,128)(2,1)S(1)} all-to-all(bf16[32,24,128]{2,1,0:T(8,128)(2,1)S(1)} %get-tuple-element.19), channel_id=1, replica_groups=mesh['row'=32,'col'=32] {'col'}, dimensions={0} | all-to-all | bytes 393216 | tf_op jit(solution)/shard_map/all_to_all | solution.py:20
  141.7 0.3 shard_map.108
  142.1 16.1 %all_to_all.46.far_ref = bf16[32,24,128]{2,1,0:T(8,128)(2,1)S(1)} all-to-all(bf16[32,24,128]{2,1,0:T(8,128)(2,1)S(1)} %get-tuple-element.21), channel_id=1, replica_groups=mesh['row'=32,'col'=32] {'row'}, dimensions={0} | all-to-all | bytes 393216 | tf_op jit(solution)/shard_map/all_to_all | solution.py:20
  158.1 3.2 %shard_map.109 = (f32[8,256]{1,0:T(8,128)}, f32[8,256]{1,0:T(8,128)}, f32[3,8,8]{2,1,0:T(8,128)}) custom-call(bf16[32,24,128]{2,1,0:T(8,128)(2,1)S(1)} %all_to_all.46.far_ref, f32[32,256]{1,0:T(8,128)S(1)} %get-tuple-element.22.state_ref), custom_call_target="tpu_custom_call" | custom-call | tf_op jit(solution)/shard_map/pallas_call | solution.py:351
  (9 shorter events, 0.0 us)
Async XLA Ops:
  0.6 0.7 copy-start.1
  1.3 45.6 %copy-start.6 = (s32[1,1,96]{2,1,0:T(1,128)S(1)}, s32[1,1,96]{2,1,0:T(1,128)}, u32[]{:S(2)}) copy-start(s32[1,1,96]{2,1,0:T(1,128)} %param.14) | copy-start | bytes 1156
  1.3 45.6 %copy-start.7 = (s32[1,1,96]{2,1,0:T(1,128)S(1)}, s32[1,1,96]{2,1,0:T(1,128)}, u32[]{:S(2)}) copy-start(s32[1,1,96]{2,1,0:T(1,128)} %param.13) | copy-start | bytes 1156
  29.7 22.9 %all-to-all-start = ((bf16[32,16,128]{2,1,0:T(8,128)(2,1)}), bf16[32,16,128]{2,1,0:T(8,128)(2,1)S(1)}, u32[]{:S(2)}, u32[]{:S(2)}) async-start(bf16[32,16,128]{2,1,0:T(8,128)(2,1)} %shard_map.103), calls=%async_computation | async-start | bytes 262144 | tf_op jit(solution)/shard_map/all_to_all | solution.py:20
  42.1 1.9 %copy-start = (bf16[1,1,96,128,128]{4,3,2,1,0:T(8,128)(2,1)S(1)}, bf16[1,1,96,128,128]{4,3,2,1,0:T(8,128)(2,1)}, u32[]{:S(2)}) copy-start(bf16[1,1,96,128,128]{4,3,2,1,0:T(8,128)(2,1)} %param.12) | copy-start | bytes 9437188
  44.0 0.7 copy-start.2
  44.7 0.7 copy-start.3
  45.4 0.7 copy-start.4
  46.0 0.7 copy-start.5

commit v7 on v6

--- a/solution.py
+++ b/solution.py
@@ -100,9 +100,7 @@
     out_ref[2 * nv :] = jnp.broadcast_to(diagonal_ref[...], (nv, out_ref.shape[1]))
 
 
-def place_products(
-    lists_ref, near_ref, far_ref, blocks_ref, near_out, far_out, near_products, far_products
-):
+def place_products(lists_ref, near_ref, far_ref, blocks_ref, near_out, far_out):
     slots = blocks_ref.shape[0]
     nv = near_out.shape[2]
 
@@ -115,43 +113,26 @@
             values = values[: 2 * nv] + values[2 * nv :]
         return values
 
-    for k in range(slots):
-        block = blocks_ref[k]
-        near_products[k] = product(far_ref, lists_ref[slots + k], block, 1)
-        far_products[k] = product(near_ref, lists_ref[k], block, 0)
     near_out[...] = jnp.zeros_like(near_out)
     far_out[...] = jnp.zeros_like(far_out)
-
-    def one_slot(k, carry):
+    live = lists_ref[2 * slots]
+    for k in range(slots):
         near, far = lists_ref[k], lists_ref[slots + k]
         near_half, far_half = near & 1, far & 1
         near_chunk, far_chunk = lax.shift_right_logical(near, 1), lax.shift_right_logical(far, 1)
-        near_out[near_chunk, near_half] += near_products[
-            k, pl.ds(pl.multiple_of(far_half * nv, nv), nv), :
-        ]
-        far_out[far_chunk, far_half] += far_products[
-            k, pl.ds(pl.multiple_of(near_half * nv, nv), nv), :
-        ]
-        return carry
-
-    lax.fori_loop(0, lists_ref[2 * slots], one_slot, 0)
+        block = blocks_ref[k]
+        near_values = product(far_ref, far, block, 1)
+        far_values = product(near_ref, near, block, 0)
+        near_values = jnp.where(far_half == 0, near_values[:nv], near_values[nv:])
+        far_values = jnp.where(near_half == 0, far_values[:nv], far_values[nv:])
+        near_out[near_chunk, near_half] += jnp.where(k < live, near_values, 0.0)
+        far_out[far_chunk, far_half] += jnp.where(k < live, far_values, 0.0)
 
 
 def first_kernel(
-    lists_ref,
-    near_ref,
-    far_ref,
-    blocks_ref,
-    near_out,
-    far_out,
-    near_products,
-    far_products,
-    near_sums,
-    far_sums,
+    lists_ref, near_ref, far_ref, blocks_ref, near_out, far_out, near_sums, far_sums
 ):
-    place_products(
-        lists_ref, near_ref, far_ref, blocks_ref, near_sums, far_sums, near_products, far_products
-    )
+    place_products(lists_ref, near_ref, far_ref, blocks_ref, near_sums, far_sums)
     for out_ref, sums_ref in ((near_out, near_sums), (far_out, far_sums)):
         for n in range(out_ref.shape[0]):
             out_ref[n] = jnp.concatenate([sums_ref[n, 0], sums_ref[n, 1]], axis=0).astype(BF16)
@@ -165,13 +146,9 @@
     state_ref,
     out_ref,
     far_out,
-    near_products,
-    far_products,
     sums_ref,
 ):
-    place_products(
-        lists_ref, near_ref, far_ref, blocks_ref, sums_ref, far_out, near_products, far_products
-    )
+    place_products(lists_ref, near_ref, far_ref, blocks_ref, sums_ref, far_out)
     nv, width = sums_ref.shape[2:]
     total = jnp.zeros((4 * nv, 4 * nv), F32)
     for n in range(out_ref.shape[0]):
@@ -307,11 +284,10 @@
     tile_blocks = blocks[0, 0]
     lists = jnp.concatenate([near_index[0, 0], far_index[0, 0], counts[0]])
     nv, share = current_block.shape
-    slots, width = tile_blocks.shape[:2]
+    width = tile_blocks.shape[1]
     n_row, n_col = lax.axis_size("row"), lax.axis_size("col")
     rows_total = share * n_row * n_col
     near_sums, far_sums = (n_col, 2, nv, width), (n_row, 2, nv, width)
-    products_scratch = [pltpu.VMEM((slots, 2 * nv, width), F32)] * 2
 
     chunks = call(rounded_kernel, shape_of((n_col, 2 * nv, width), BF16), [VMEM])(current_block)
     constants, held_blocks = call(
@@ -323,7 +299,7 @@
         first_kernel,
         (shape_of((n_col, 2 * nv, width), BF16), shape_of((n_row, 2 * nv, width), BF16)),
         [SMEM, VMEM, VMEM, VMEM],
-        products_scratch + [pltpu.VMEM(near_sums, F32), pltpu.VMEM(far_sums, F32)],
+        [pltpu.VMEM(near_sums, F32), pltpu.VMEM(far_sums, F32)],
     )(lists, near_vectors, far_vectors, held_blocks)
     far_got = exchange(far_part, "row")
     near_got = exchange(near_part, "col")
@@ -339,7 +315,7 @@
         second_kernel,
         (shape_of((n_col, 3 * nv, width), BF16), shape_of(far_sums)),
         [SMEM, VMEM, VMEM, VMEM, VMEM],
-        products_scratch + [pltpu.VMEM(near_sums, F32)],
+        [pltpu.VMEM(near_sums, F32)],
     )(lists, near_vectors, far_vectors, held_blocks, state)
     near_got = exchange(near_part, "col")
     late, far_part = call(

time: 162 us -> 160 us (0.988)
  no operation moved by 1% of the time
where the time goes in v7:
time: 160 us
  blocking collectives  123 us (77%)
  Pallas kernels  12.1 us (8%)
  starting transfers between devices  11.7 us (7%)
  waiting for transfers between devices  5.63 us (4%)
  local copies, waits for them, and re-layouts  5.34 us (3%)
    all_to_all x7, blocking collectives, exchange(): return lax.all_to_all(chunks, axis, split_axis=0, concat_axis=0, tiled=True)  123 us
    all_to_all x1, starting transfers between devices, exchange(): return lax.all_to_all(chunks, axis, split_axis=0, concat_axis=0, tiled=True)  11.7 us
    all_to_all x1, waiting for transfers between devices, exchange(): return lax.all_to_all(chunks, axis, split_axis=0, concat_axis=0, tiled=True)  5.63 us
    unnamed x16, local copies, waits for them, and re-layouts  5.34 us
    pallas_call x1, Pallas kernels, on_device(): call(second_kernel, (shape_of((n_col, 3 * nv, width), BF16), shape_of(far...  4.21 us
    pallas_call x1, Pallas kernels, on_device(): call(first_kernel, (shape_of((n_col, 2 * nv, width), BF16), shape_of((n_r...  3.28 us
  transfers between devices with their start and end apart: 1, of which 1 were waited for; matrix products, arithmetic and copies ran while one was open for 0% of the time, Pallas kernels for 0%

profile of v7, /device:TPU:1, one launch (start us, length us, event | category | flops | bytes accessed | tf_op | source)
XLA Modules:
  0.0 159.7 jit_solution(15972391337847829405)
XLA Ops:
  0.6 0.0 copy-start.1
  0.6 0.7 copy-done.1
  1.3 0.7 shard_map.103
  2.0 27.7 %all_to_all.40.far_ref = bf16[32,16,128]{2,1,0:T(8,128)(2,1)S(1)} all-to-all(bf16[32,16,128]{2,1,0:T(8,128)(2,1)} %shard_map.103), channel_id=1, replica_groups=mesh['row'=32,'col'=32] {'row'}, dimensions={0} | all-to-all | bytes 262144 | tf_op jit(solution)/shard_map/all_to_all | solution.py:20
  29.7 11.7 %all-to-all-start = ((bf16[32,16,128]{2,1,0:T(8,128)(2,1)}), bf16[32,16,128]{2,1,0:T(8,128)(2,1)S(1)}, u32[]{:S(2)}, u32[]{:S(2)}) async-start(bf16[32,16,128]{2,1,0:T(8,128)(2,1)} %shard_map.103), calls=%async_computation | async-start | bytes 262144 | tf_op jit(solution)/shard_map/all_to_all | solution.py:20
  42.1 1.9 %copy-done = bf16[1,1,96,128,128]{4,3,2,1,0:T(8,128)(2,1)S(1)} copy-done((bf16[1,1,96,128,128]{4,3,2,1,0:T(8,128)(2,1)S(1)}, bf16[1,1,96,128,128]{4,3,2,1,0:T(8,128)(2,1)}, u32[]{:S(2)}) %copy-start) | copy-done | bytes 3145752
  44.0 0.7 copy-done.2
  44.7 0.7 copy-done.3
  45.4 0.7 copy-done.4
  46.1 0.7 copy-done.5
  46.7 0.2 shard_map.104
  47.0 0.1 pad_add_fusion.lists_ref
  47.0 5.6 %all-to-all-done.near_ref = bf16[32,16,128]{2,1,0:T(8,128)(2,1)S(1)} async-done(((bf16[32,16,128]{2,1,0:T(8,128)(2,1)}), bf16[32,16,128]{2,1,0:T(8,128)(2,1)S(1)}, u32[]{:S(2)}, u32[]{:S(2)}) %all-to-all-start) | async-done | bytes 131104 | tf_op jit(solution)/shard_map/all_to_all | solution.py:20
  52.7 3.3 %shard_map.105 = (bf16[32,16,128]{2,1,0:T(8,128)(2,1)S(1)}, bf16[32,16,128]{2,1,0:T(8,128)(2,1)S(1)}) custom-call(s32[193]{0:T(256)S(1)} %pad_add_fusion.lists_ref, bf16[32,16,128]{2,1,0:T(8,128)(2,1)S(1)} %all-to-all-done.near_ref, bf16[32,16,128]{2,1,0:T(8,128)(2,1)S(1)} %all_to_all.40.far_ref, bf16[96,128,128]{2,1,0:T(8,128)(2,1)S(1)} %get-tuple-element.13.blocks_ref), custom_call_target="tpu_custom_call" | custom-call | tf_op jit(solution)/shard_map/pallas_call | solution.py:298
  56.0 17.0 %all_to_all.41.near_ref = bf16[32,16,128]{2,1,0:T(8,128)(2,1)S(1)} all-to-all(bf16[32,16,128]{2,1,0:T(8,128)(2,1)S(1)} %get-tuple-element.14), channel_id=1, replica_groups=mesh['row'=32,'col'=32] {'col'}, dimensions={0} | all-to-all | bytes 262144 | tf_op jit(solution)/shard_map/all_to_all | solution.py:20
  73.0 14.7 %all_to_all.42.far_ref = bf16[32,16,128]{2,1,0:T(8,128)(2,1)S(1)} all-to-all(bf16[32,16,128]{2,1,0:T(8,128)(2,1)S(1)} %get-tuple-element.15), channel_id=1, replica_groups=mesh['row'=32,'col'=32] {'row'}, dimensions={0} | all-to-all | bytes 262144 | tf_op jit(solution)/shard_map/all_to_all | solution.py:20
  87.7 0.3 shard_map.106
  87.9 15.2 %all_to_all.43.far_ref = bf16[32,32,128]{2,1,0:T(8,128)(2,1)S(1)} all-to-all(bf16[32,32,128]{2,1,0:T(8,128)(2,1)S(1)} %get-tuple-element.17), channel_id=1, replica_groups=mesh['row'=32,'col'=32] {'row'}, dimensions={0} | all-to-all | bytes 524288 | tf_op jit(solution)/shard_map/all_to_all | solution.py:20
  103.2 14.8 %all_to_all.44.near_ref = bf16[32,32,128]{2,1,0:T(8,128)(2,1)S(1)} all-to-all(bf16[32,32,128]{2,1,0:T(8,128)(2,1)S(1)} %get-tuple-element.17), channel_id=1, replica_groups=mesh['row'=32,'col'=32] {'col'}, dimensions={0} | all-to-all | bytes 524288 | tf_op jit(solution)/shard_map/all_to_all | solution.py:20
  118.0 4.2 %shard_map.107 = (bf16[32,24,128]{2,1,0:T(8,128)(2,1)S(1)}, f32[32,2,8,128]{3,2,1,0:T(8,128)S(1)}) custom-call(s32[193]{0:T(256)S(1)} %pad_add_fusion.lists_ref, bf16[32,32,128]{2,1,0:T(8,128)(2,1)S(1)} %all_to_all.44.near_ref, bf16[32,32,128]{2,1,0:T(8,128)(2,1)S(1)} %all_to_all.43.far_ref, bf16[96,128,128]{2,1,0:T(8,128)(2,1)S(1)} %get-tuple-element.13.blocks_ref, ...), custom_call_target="tpu_custom_call" | custom-call | tf_op jit(solution)/shard_map/pallas_call | solution.py:314
  122.2 17.9 %all_to_all.45.near_ref = bf16[32,24,128]{2,1,0:T(8,128)(2,1)S(1)} all-to-all(bf16[32,24,128]{2,1,0:T(8,128)(2,1)S(1)} %get-tuple-element.19), channel_id=1, replica_groups=mesh['row'=32,'col'=32] {'col'}, dimensions={0} | all-to-all | bytes 393216 | tf_op jit(solution)/shard_map/all_to_all | solution.py:20
  140.1 0.3 shard_map.108
  140.4 16.1 %all_to_all.46.far_ref = bf16[32,24,128]{2,1,0:T(8,128)(2,1)S(1)} all-to-all(bf16[32,24,128]{2,1,0:T(8,128)(2,1)S(1)} %get-tuple-element.21), channel_id=1, replica_groups=mesh['row'=32,'col'=32] {'row'}, dimensions={0} | all-to-all | bytes 393216 | tf_op jit(solution)/shard_map/all_to_all | solution.py:20
  156.5 3.2 %shard_map.109 = (f32[8,256]{1,0:T(8,128)}, f32[8,256]{1,0:T(8,128)}, f32[3,8,8]{2,1,0:T(8,128)}) custom-call(bf16[32,24,128]{2,1,0:T(8,128)(2,1)S(1)} %all_to_all.46.far_ref, f32[32,256]{1,0:T(8,128)S(1)} %get-tuple-element.22.state_ref), custom_call_target="tpu_custom_call" | custom-call | tf_op jit(solution)/shard_map/pallas_call | solution.py:327
  (9 shorter events, 0.0 us)
Async XLA Ops:
  0.6 0.7 copy-start.1
  1.3 45.6 %copy-start.6 = (s32[1,1,96]{2,1,0:T(1,128)S(1)}, s32[1,1,96]{2,1,0:T(1,128)}, u32[]{:S(2)}) copy-start(s32[1,1,96]{2,1,0:T(1,128)} %param.14) | copy-start | bytes 1156
  1.3 45.6 %copy-start.7 = (s32[1,1,96]{2,1,0:T(1,128)S(1)}, s32[1,1,96]{2,1,0:T(1,128)}, u32[]{:S(2)}) copy-start(s32[1,1,96]{2,1,0:T(1,128)} %param.13) | copy-start | bytes 1156
  29.7 22.9 %all-to-all-start = ((bf16[32,16,128]{2,1,0:T(8,128)(2,1)}), bf16[32,16,128]{2,1,0:T(8,128)(2,1)S(1)}, u32[]{:S(2)}, u32[]{:S(2)}) async-start(bf16[32,16,128]{2,1,0:T(8,128)(2,1)} %shard_map.103), calls=%async_computation | async-start | bytes 262144 | tf_op jit(solution)/shard_map/all_to_all | solution.py:20
  42.1 1.9 %copy-start = (bf16[1,1,96,128,128]{4,3,2,1,0:T(8,128)(2,1)S(1)}, bf16[1,1,96,128,128]{4,3,2,1,0:T(8,128)(2,1)}, u32[]{:S(2)}) copy-start(bf16[1,1,96,128,128]{4,3,2,1,0:T(8,128)(2,1)} %param.12) | copy-start | bytes 9437188
  44.0 0.7 copy-start.2
  44.7 0.7 copy-start.3
  45.4 0.7 copy-start.4
  46.0 0.7 copy-start.5

commit v8 on v7

--- a/solution.py
+++ b/solution.py
@@ -309,8 +309,9 @@
         [VMEM] * 3,
     )(near_got, far_got, constants)
 
+    near_vectors = exchange(chunks, "col")
+    chunks, near_vectors = lax.optimization_barrier((chunks, near_vectors))
     far_vectors = exchange(chunks, "row")
-    near_vectors = exchange(chunks, "col")
     near_part, far_part = call(
         second_kernel,
         (shape_of((n_col, 3 * nv, width), BF16), shape_of(far_sums)),

time: 160 us -> 161 us (level)
  no operation moved by 1% of the time
where the time goes in v8:
time: 161 us; the launch traced here: 160 us
  blocking collectives  124 us (77%)
  Pallas kernels  12.1 us (8%)
  starting transfers between devices  11.7 us (7%)
  waiting for transfers between devices  5.63 us (3%)
  local copies, waits for them, and re-layouts  5.34 us (3%)
    all_to_all x7, blocking collectives, exchange(): return lax.all_to_all(chunks, axis, split_axis=0, concat_axis=0, tiled=True)  124 us
    all_to_all x1, starting transfers between devices, exchange(): return lax.all_to_all(chunks, axis, split_axis=0, concat_axis=0, tiled=True)  11.7 us
    all_to_all x1, waiting for transfers between devices, exchange(): return lax.all_to_all(chunks, axis, split_axis=0, concat_axis=0, tiled=True)  5.63 us
    unnamed x16, local copies, waits for them, and re-layouts  5.34 us
    pallas_call x1, Pallas kernels, on_device(): call(second_kernel, (shape_of((n_col, 3 * nv, width), BF16), shape_of(far...  4.2 us
    pallas_call x1, Pallas kernels, on_device(): call(first_kernel, (shape_of((n_col, 2 * nv, width), BF16), shape_of((n_r...  3.28 us
  transfers between devices with their start and end apart: 1, of which 1 were waited for; matrix products, arithmetic and copies ran while one was open for 0% of the time, Pallas kernels for 0%

profile of v8, /device:TPU:1, one launch (start us, length us, event | category | flops | bytes accessed | tf_op | source)
XLA Modules:
  0.0 159.9 jit_solution(6109640283247305059)
XLA Ops:
  0.6 0.7 copy-done.1
  1.3 0.7 shard_map.103
  2.0 27.7 %all_to_all.40.far_ref = bf16[32,16,128]{2,1,0:T(8,128)(2,1)S(1)} all-to-all(bf16[32,16,128]{2,1,0:T(8,128)(2,1)} %shard_map.103), channel_id=1, replica_groups=mesh['row'=32,'col'=32] {'row'}, dimensions={0} | all-to-all | bytes 262144 | tf_op jit(solution)/shard_map/all_to_all | solution.py:20
  29.7 11.7 %all-to-all-start = ((bf16[32,16,128]{2,1,0:T(8,128)(2,1)}), bf16[32,16,128]{2,1,0:T(8,128)(2,1)S(1)}, u32[]{:S(2)}, u32[]{:S(2)}) async-start(bf16[32,16,128]{2,1,0:T(8,128)(2,1)} %shard_map.103), calls=%async_computation | async-start | bytes 262144 | tf_op jit(solution)/shard_map/all_to_all | solution.py:20
  42.1 0.0 copy-start
  42.1 1.9 %copy-done = bf16[1,1,96,128,128]{4,3,2,1,0:T(8,128)(2,1)S(1)} copy-done((bf16[1,1,96,128,128]{4,3,2,1,0:T(8,128)(2,1)S(1)}, bf16[1,1,96,128,128]{4,3,2,1,0:T(8,128)(2,1)}, u32[]{:S(2)}) %copy-start) | copy-done | bytes 3145752
  44.0 0.7 copy-done.2
  44.7 0.7 copy-done.3
  45.4 0.7 copy-done.4
  46.1 0.7 copy-done.5
  46.7 0.2 shard_map.104
  47.0 0.1 pad_add_fusion.lists_ref
  47.0 5.6 %all-to-all-done.near_ref = bf16[32,16,128]{2,1,0:T(8,128)(2,1)S(1)} async-done(((bf16[32,16,128]{2,1,0:T(8,128)(2,1)}), bf16[32,16,128]{2,1,0:T(8,128)(2,1)S(1)}, u32[]{:S(2)}, u32[]{:S(2)}) %all-to-all-start) | async-done | bytes 131104 | tf_op jit(solution)/shard_map/all_to_all | solution.py:20
  52.7 3.3 %shard_map.105 = (bf16[32,16,128]{2,1,0:T(8,128)(2,1)S(1)}, bf16[32,16,128]{2,1,0:T(8,128)(2,1)S(1)}) custom-call(s32[193]{0:T(256)S(1)} %pad_add_fusion.lists_ref, bf16[32,16,128]{2,1,0:T(8,128)(2,1)S(1)} %all-to-all-done.near_ref, bf16[32,16,128]{2,1,0:T(8,128)(2,1)S(1)} %all_to_all.40.far_ref, bf16[96,128,128]{2,1,0:T(8,128)(2,1)S(1)} %get-tuple-element.15.blocks_ref), custom_call_target="tpu_custom_call" | custom-call | tf_op jit(solution)/shard_map/pallas_call | solution.py:298
  56.0 17.0 %all_to_all.41.near_ref = bf16[32,16,128]{2,1,0:T(8,128)(2,1)S(1)} all-to-all(bf16[32,16,128]{2,1,0:T(8,128)(2,1)S(1)} %get-tuple-element.16), channel_id=1, replica_groups=mesh['row'=32,'col'=32] {'col'}, dimensions={0} | all-to-all | bytes 262144 | tf_op jit(solution)/shard_map/all_to_all | solution.py:20
  73.0 14.7 %all_to_all.42.far_ref = bf16[32,16,128]{2,1,0:T(8,128)(2,1)S(1)} all-to-all(bf16[32,16,128]{2,1,0:T(8,128)(2,1)S(1)} %get-tuple-element.17), channel_id=1, replica_groups=mesh['row'=32,'col'=32] {'row'}, dimensions={0} | all-to-all | bytes 262144 | tf_op jit(solution)/shard_map/all_to_all | solution.py:20
  87.7 0.3 shard_map.106
  87.9 14.6 %all_to_all.43.near_ref = bf16[32,32,128]{2,1,0:T(8,128)(2,1)S(1)} all-to-all(bf16[32,32,128]{2,1,0:T(8,128)(2,1)S(1)} %get-tuple-element.21), channel_id=1, replica_groups=mesh['row'=32,'col'=32] {'col'}, dimensions={0} | all-to-all | bytes 524288 | tf_op jit(solution)/shard_map/all_to_all | solution.py:20
  102.6 18.5 %all_to_all.44.far_ref = bf16[32,32,128]{2,1,0:T(8,128)(2,1)S(1)} all-to-all(bf16[32,32,128]{2,1,0:T(8,128)(2,1)S(1)} %get-tuple-element.21), channel_id=1, replica_groups=mesh['row'=32,'col'=32] {'row'}, dimensions={0} | all-to-all | bytes 524288 | tf_op jit(solution)/shard_map/all_to_all | solution.py:20
  121.1 4.2 %shard_map.107 = (bf16[32,24,128]{2,1,0:T(8,128)(2,1)S(1)}, f32[32,2,8,128]{3,2,1,0:T(8,128)S(1)}) custom-call(s32[193]{0:T(256)S(1)} %pad_add_fusion.lists_ref, bf16[32,32,128]{2,1,0:T(8,128)(2,1)S(1)} %all_to_all.43.near_ref, bf16[32,32,128]{2,1,0:T(8,128)(2,1)S(1)} %all_to_all.44.far_ref, bf16[96,128,128]{2,1,0:T(8,128)(2,1)S(1)} %get-tuple-element.15.blocks_ref, ...), custom_call_target="tpu_custom_call" | custom-call | tf_op jit(solution)/shard_map/pallas_call | solution.py:315
  125.3 15.2 %all_to_all.45.near_ref = bf16[32,24,128]{2,1,0:T(8,128)(2,1)S(1)} all-to-all(bf16[32,24,128]{2,1,0:T(8,128)(2,1)S(1)} %get-tuple-element.23), channel_id=1, replica_groups=mesh['row'=32,'col'=32] {'col'}, dimensions={0} | all-to-all | bytes 393216 | tf_op jit(solution)/shard_map/all_to_all | solution.py:20
  140.5 0.3 shard_map.108
  140.9 15.9 %all_to_all.46.far_ref = bf16[32,24,128]{2,1,0:T(8,128)(2,1)S(1)} all-to-all(bf16[32,24,128]{2,1,0:T(8,128)(2,1)S(1)} %get-tuple-element.25), channel_id=1, replica_groups=mesh['row'=32,'col'=32] {'row'}, dimensions={0} | all-to-all | bytes 393216 | tf_op jit(solution)/shard_map/all_to_all | solution.py:20
  156.8 3.2 %shard_map.109 = (f32[8,256]{1,0:T(8,128)}, f32[8,256]{1,0:T(8,128)}, f32[3,8,8]{2,1,0:T(8,128)}) custom-call(bf16[32,24,128]{2,1,0:T(8,128)(2,1)S(1)} %all_to_all.46.far_ref, f32[32,256]{1,0:T(8,128)S(1)} %get-tuple-element.26.state_ref), custom_call_target="tpu_custom_call" | custom-call | tf_op jit(solution)/shard_map/pallas_call | solution.py:328
  (9 shorter events, 0.0 us)
Async XLA Ops:
  0.6 0.7 copy-start.1
  1.3 45.6 %copy-start.6 = (s32[1,1,96]{2,1,0:T(1,128)S(1)}, s32[1,1,96]{2,1,0:T(1,128)}, u32[]{:S(2)}) copy-start(s32[1,1,96]{2,1,0:T(1,128)} %param.14) | copy-start | bytes 1156
  1.3 45.6 %copy-start.7 = (s32[1,1,96]{2,1,0:T(1,128)S(1)}, s32[1,1,96]{2,1,0:T(1,128)}, u32[]{:S(2)}) copy-start(s32[1,1,96]{2,1,0:T(1,128)} %param.13) | copy-start | bytes 1156
  29.7 22.9 %all-to-all-start = ((bf16[32,16,128]{2,1,0:T(8,128)(2,1)}), bf16[32,16,128]{2,1,0:T(8,128)(2,1)S(1)}, u32[]{:S(2)}, u32[]{:S(2)}) async-start(bf16[32,16,128]{2,1,0:T(8,128)(2,1)} %shard_map.103), calls=%async_computation | async-start | bytes 262144 | tf_op jit(solution)/shard_map/all_to_all | solution.py:20
  42.1 1.9 %copy-start = (bf16[1,1,96,128,128]{4,3,2,1,0:T(8,128)(2,1)S(1)}, bf16[1,1,96,128,128]{4,3,2,1,0:T(8,128)(2,1)}, u32[]{:S(2)}) copy-start(bf16[1,1,96,128,128]{4,3,2,1,0:T(8,128)(2,1)} %param.12) | copy-start | bytes 9437188
  44.0 0.7 copy-start.2
  44.7 0.7 copy-start.3
  45.4 0.7 copy-start.4
  46.0 0.7 copy-start.5
